TPU v7x, 32 devices: a whole 2x2x4 slice. The times are simulated.
32 devices in a mesh: row: 8 (over z, core), col: 4 (over y, x).
Axes of the slice: x: 2, y: 2, z: 4, core: 2. Of those that a mesh axis runs over, the one named last changes fastest.
Arguments:
- eigvec: float32 [16384, 8192], P('row', 'col'), may hold values from -6 to 6
- slots: float32 [4, 16384, 256], P('col', 'row'), may hold values from -0.046875 to 0.046875
- roots: int32 [3], replicated, may hold values from 0 to 3, as said below
- tfac: float32 [3, 256, 256], replicated, as said below
Outputs:
- transformed: float32 [16384, 8192], P('row', 'col')
Inputs may be any that keep to these rules, and one draw needn't show every extreme that they name: The panels lie in consecutive grid columns, roots[k] = (roots[0] + k) mod 4; roots[0] is one of the last two grid columns, so the panels always wrap past the last grid column. tfac[k] is upper triangular with a diagonal between 1 and 2.
All inputs are finite; a program needn't handle non-finite values.
Results may differ from a plain program's by a relative error of at most 0.00013.
Values sent between devices are 32-bit elements; how exact they have to be, the bound alone decides.
No kernel may reach another device: no remote copies, remote signals or barrier semaphores. Data moves between devices by JAX's collectives and lax.ppermute only.
A program may use at most 128 MiB of HBM per device.

v0:
```python
import functools

import jax
import jax.numpy as jnp
from jax import lax
from jax.experimental import pallas as pl
from jax.experimental.pallas import tpu as pltpu
from jax.sharding import PartitionSpec as P

PANELS = 3
BLOCK = 512
VMEM = 40 * 1024 * 1024
F32 = jnp.float32
BF16 = jnp.bfloat16
ANYWHERE = pl.BlockSpec(memory_space=pl.ANY)


def split(value):
    high = value.astype(BF16)
    return high, (value - high.astype(F32)).astype(BF16)


def dot(left, right):
    return jnp.dot(left, right, preferred_element_type=F32)


def dot_three(left, right):
    left_high, left_low = split(left)
    right_high, right_low = split(right)
    return dot(left_high, right_high) + (dot(left_high, right_low) + dot(left_low, right_high))


def params():
    return pltpu.CompilerParams(vmem_limit_bytes=VMEM)


def cost(flops, count):
    return pl.CostEstimate(flops=flops // 64, bytes_accessed=count // 64, transcendentals=0)


def split_kernel(x_ref, high_ref, low_ref):
    high_ref[...], low_ref[...] = split(x_ref[...])


def split_array(x):
    rows, columns = x.shape
    step = min(rows, 256)
    spec = pl.BlockSpec((step, columns), lambda i: (i, 0))
    return pl.pallas_call(
        split_kernel,
        grid=(rows // step,),
        in_specs=[spec],
        out_specs=[spec, spec],
        out_shape=[jax.ShapeDtypeStruct(x.shape, BF16)] * 2,
        compiler_params=params(),
        cost_estimate=cost(rows * columns * 4, rows * columns * 8),
        name="split_x",
    )(x)


def prepare_kernel(keep_ref, send_ref, *refs):
    high_ref, low_ref, flipped_ref = refs[-3:]
    both = jnp.concatenate([keep_ref[...], send_ref[...]], axis=1)
    high_ref[...], low_ref[...] = split(both)
    high, low = split(both.T)
    width = both.shape[1]
    flipped_ref[:width, :] = high
    flipped_ref[width:, :] = low


def prepare(keep, send, after=()):
    rows, half = keep.shape
    step = min(rows, 512)
    half_spec = pl.BlockSpec((step, half), lambda i: (i, 0))
    spec = pl.BlockSpec((step, 2 * half), lambda i: (i, 0))
    return pl.pallas_call(
        prepare_kernel,
        grid=(rows // step,),
        in_specs=[half_spec, half_spec] + [ANYWHERE] * len(after),
        out_specs=[spec, spec, pl.BlockSpec((4 * half, step), lambda i: (0, i))],
        out_shape=[
            jax.ShapeDtypeStruct((rows, 2 * half), BF16),
            jax.ShapeDtypeStruct((rows, 2 * half), BF16),
            jax.ShapeDtypeStruct((4 * half, rows), BF16),
        ],
        compiler_params=params(),
        cost_estimate=cost(rows * half * 8, rows * half * 24),
        name="prepare_panel",
    )(keep, send, *after)


def products_kernel(flipped_ref, high_ref, low_ref, *refs):
    keep_ref, send_ref = refs[-2:]
    width = flipped_ref.shape[0] // 2
    with_high = dot(flipped_ref[...], high_ref[...])
    with_low = dot(flipped_ref[:width, :], low_ref[...])
    total = with_high[:width] + (with_high[width:] + with_low)
    keep_ref[...] = total[: width // 2]
    send_ref[...] = total[width // 2 :]


def products(flipped, high, low, block, width, after=()):
    rows = high.shape[0]
    half = flipped.shape[0] // 4
    step = min(width, 256)
    steps = width // step
    x_spec = pl.BlockSpec((rows, step), lambda i: (0, block * steps + i))
    out_spec = pl.BlockSpec((half, step), lambda i: (0, i))
    return pl.pallas_call(
        products_kernel,
        grid=(steps,),
        in_specs=[pl.BlockSpec((4 * half, rows), lambda i: (0, 0)), x_spec, x_spec]
        + [ANYWHERE] * len(after),
        out_specs=[out_spec, out_spec],
        out_shape=[jax.ShapeDtypeStruct((half, width), F32)] * 2,
        compiler_params=params(),
        cost_estimate=cost(2 * 6 * half * rows * width, rows * width * 4 + 8 * half * rows),
        name="products",
    )(flipped, high, low, *after)


def update_kernel(place_ref, *refs):
    sums = refs[:6]
    tfac_ref, gram_ref = refs[6:8]
    high_refs, low_refs = refs[8:11], refs[11:14]
    x_ref = refs[14]
    out_ref, w_ref, y_ref, y_high_ref, y_low_ref = refs[-5:]
    half = sums[0].shape[0]
    width = 2 * half

    @pl.when(pl.program_id(0) == 0)
    def _():
        for index, piece in enumerate(sums):
            start = pl.multiple_of(place_ref[index] * half, half)
            w_ref[pl.ds(start, half), :] = piece[...]
        first = dot_three(tfac_ref[0], w_ref[:width, :])
        y_ref[:width, :] = first
        second = dot_three(tfac_ref[1], w_ref[width : 2 * width, :] - dot_three(gram_ref[0], first))
        y_ref[width : 2 * width, :] = second
        third = w_ref[2 * width :, :] - dot_three(gram_ref[1], first) - dot_three(gram_ref[2], second)
        y_ref[2 * width :, :] = dot_three(tfac_ref[2], third)
        for index in range(6):
            start = pl.multiple_of(place_ref[index] * half, half)
            high, low = split(y_ref[pl.ds(start, half), :])
            y_high_ref[index * half : (index + 1) * half, :] = high
            y_low_ref[index * half : (index + 1) * half, :] = low

    high = jnp.concatenate([ref[...] for ref in high_refs], axis=1)
    low = jnp.concatenate([ref[...] for ref in low_refs], axis=1)
    change = dot(high, y_high_ref[...]) + (dot(high, y_low_ref[...]) + dot(low, y_high_ref[...]))
    out_ref[...] = x_ref[...] - change


def update(place, sums, tfac, grams, highs, lows, x, out, block, width):
    rows, columns = x.shape
    half = sums[0].shape[0]
    step = min(rows, 512)
    whole = lambda *shape: pl.BlockSpec(shape, lambda i, place: (0,) * len(shape))
    panel_spec = pl.BlockSpec((step, 2 * half), lambda i, place: (i, 0))
    block_spec = pl.BlockSpec((step, width), lambda i, place: (i, block))
    operands = [place, *sums, tfac, grams, *highs, *lows, x]
    in_specs = (
        [whole(half, width)] * 6
        + [whole(3, 2 * half, 2 * half)] * 2
        + [panel_spec] * 6
        + [block_spec]
    )
    aliases = {}
    if out is not None:
        aliases = {len(operands): 0}
        operands.append(out)
        in_specs.append(pl.BlockSpec(memory_space=pl.ANY))
    return pl.pallas_call(
        update_kernel,
        grid_spec=pltpu.PrefetchScalarGridSpec(
            num_scalar_prefetch=1,
            grid=(rows // step,),
            in_specs=in_specs,
            out_specs=block_spec,
            scratch_shapes=[
                pltpu.VMEM((6 * half, width), F32),
                pltpu.VMEM((6 * half, width), F32),
                pltpu.VMEM((6 * half, width), BF16),
                pltpu.VMEM((6 * half, width), BF16),
            ],
        ),
        out_shape=jax.ShapeDtypeStruct(x.shape, F32),
        input_output_aliases=aliases,
        compiler_params=params(),
        cost_estimate=cost(2 * 18 * half * rows * width, rows * width * 8 + rows * half * 24),
        name="update",
    )(*operands)


def pairs_of(count, step):
    return [(index, index ^ step) for index in range(count)]


def swap_cores(value):
    return lax.ppermute(value, "row", pairs_of(lax.axis_size("row"), 1))


def both_cores(chip_pairs):
    return [(2 * a + core, 2 * b + core) for a, b in chip_pairs for core in range(2)]


def sum_over_rows(keep, send):
    chips = lax.axis_size("row") // 2
    chip = lax.axis_index("row") // 2
    total = keep + swap_cores(send)
    for hop in range(chips // 2 - 1):
        pairs = [(hop, hop + 1), (chips - 1 - hop, chips - 2 - hop)]
        total = total + lax.ppermute(total, "row", both_cores(pairs))
    middle = [(chips // 2 - 1, chips // 2), (chips // 2, chips // 2 - 1)]
    total = total + lax.ppermute(total, "row", both_cores(middle))
    for hop in reversed(range(chips // 2 - 1)):
        pairs = [(hop + 1, hop), (chips - 2 - hop, chips - 1 - hop)]
        arrived = lax.ppermute(total, "row", both_cores(pairs))
        total = jnp.where((chip == hop) | (chip == chips - 1 - hop), arrived, total)
    return total, swap_cores(total)


def pick(index, *cases):
    return lax.select_n(index, *cases)


def fetch_square(slot, roots):
    half = slot.shape[1] // 2
    me = lax.axis_index("col")
    along = lambda value, step: lax.ppermute(value, "col", pairs_of(4, step))
    own = [slot[:, :half], slot[:, half:]]
    near, far = [], []
    for piece in own:
        near.append(along(piece, 1))
        far.append(along(piece, 2))
    cross = [along(far[0], 1), along(near[1], 2)]
    spare = (roots[0] + 3) % 4
    case = me ^ spare
    rounds = [
        (pick(case, near[0], own[0], own[0], own[0]), pick(case, far[0], own[1], own[1], own[1])),
        (pick(case, near[1], far[0], near[0], near[0]), pick(case, far[1], far[1], near[1], far[0])),
        (pick(case, cross[0], cross[0], cross[0], near[1]), pick(case, cross[1], cross[1], cross[1], far[1])),
    ]
    slots = jnp.array([[1, 2, 1, 2, 3, 3], [0, 0, 2, 2, 3, 3], [0, 0, 1, 1, 3, 3], [0, 0, 1, 2, 1, 2]], jnp.int32)
    halves = jnp.array([[0, 0, 1, 1, 0, 1], [0, 1, 0, 1, 0, 1], [0, 1, 0, 1, 0, 1], [0, 1, 0, 0, 1, 1]], jnp.int32)
    panel = ((slots[case] ^ me) - roots[0]) % 4
    places = panel * 2 + halves[case]
    later_of = jnp.array([[0, 1, 0, 0], [1, 0, 2, 2]], jnp.int32)[roots[0] - 2, me]
    earlier_of = jnp.array([[2, 2, 0, 1], [0, 0, 1, 0]], jnp.int32)[roots[0] - 2, me]
    later = [pick(later_of, own[h], near[h], far[h]) for h in range(2)]
    earlier = [pick(earlier_of, own[h], near[h], far[h]) for h in range(2)]
    holders = jnp.array([[3, 0, 1], [2, 3, 0]], jnp.int32)[roots[0] - 2]
    return rounds, places, later, earlier, holders


def fetch_any(slot, roots):
    half = slot.shape[1] // 2
    me = lax.axis_index("col")
    panels = [lax.psum(jnp.where(me == roots[index], slot, jnp.zeros_like(slot)), "col") for index in range(PANELS)]
    rounds = [(panel[:, :half], panel[:, half:]) for panel in panels]
    return rounds, jnp.arange(2 * PANELS, dtype=jnp.int32), panels


def gram(left, right):
    return lax.dot_general(
        left, right, (((0,), (0,)), ((), ())), precision=lax.Precision.HIGH, preferred_element_type=F32
    )


def exchange_kernel(step, ends_ref, *refs):
    names, refs = step, list(refs)
    use = dict(zip(names, refs))
    end = ends_ref[0] == 1
    if "acc" in use:
        use["acc"][...] = use["keep"][...] + use["swapped"][...]
    if "part" in use:
        columns = use["part"].shape[1]
        use["part"][...] = use["acc_before"][...] + use["outer"][:, :columns]
    if "total" in use:
        use["total"][...] = use["part_before"][...] + use["inner"][...]
    if "final" in use:
        columns = use["final"].shape[1]
        use["final"][...] = jnp.where(end, use["outer"][:, :columns], use["total_before"][...])
    if "out" in use:
        sources = [use[name] for name in ("acc", "total") if name in use]
        if len(sources) == 1:
            use["out"][...] = sources[0][...]
        else:
            both = min(source.shape[1] for source in sources)
            use["out"][:, :both] = jnp.where(end, sources[0][:, :both], sources[1][:, :both])
            for source in sources:
                if source.shape[1] > both:
                    use["out"][:, both:] = source[:, both:]


def exchange(ends, operands, shapes):
    names = list(operands) + list(shapes)
    in_vmem = pl.BlockSpec(memory_space=pltpu.VMEM)
    results = pl.pallas_call(
        functools.partial(exchange_kernel, names),
        in_specs=[pl.BlockSpec(memory_space=pltpu.SMEM)] + [in_vmem] * len(operands),
        out_specs=[in_vmem] * len(shapes),
        out_shape=[jax.ShapeDtypeStruct(shape, F32) for shape in shapes.values()],
        compiler_params=params(),
        cost_estimate=cost(0, 0),
        name="exchange",
    )(ends, *operands.values())
    return dict(zip(shapes, results))


def shards_square(eigvec, slot, roots, tfac):
    columns = eigvec.shape[1]
    width = columns // 2
    rounds, places, later, earlier, holders = fetch_square(slot, roots)
    chip, core = lax.axis_index("row") // 2, lax.axis_index("row") % 2
    ends = jnp.where((chip == 0) | (chip == 3), 1, 0).astype(jnp.int32).reshape(1)
    places = jnp.where(core == 0, places, places.reshape(PANELS, 2)[:, ::-1].reshape(-1))
    ordered = lambda pair: (jnp.where(core == 0, *pair), jnp.where(core == 0, *pair[::-1]))
    x_high, x_low = split_array(eigvec)
    chunks = [(index, block) for index in range(PANELS) for block in range(columns // width)]
    count = len(chunks)
    gram_chunk = 3
    prepared, keep, swapped, sizes = {}, {}, {}, {}

    def start(number, after):
        index, block = chunks[number]
        if index not in prepared:
            prepared[index] = prepare(*ordered(rounds[index]), after)
        mine, other = products(prepared[index][2], x_high, x_low, block, width, after)
        if number == gram_chunk:
            flipped = prepare(*ordered(later), after)[2]
            high, low, _ = prepare(*earlier, after)
            extra = products(flipped, high, low, 0, high.shape[1])
            mine = jnp.concatenate([mine, extra[0]], axis=1)
            other = jnp.concatenate([other, extra[1]], axis=1)
        keep[number], swapped[number], sizes[number] = mine, swap_cores(other), mine.shape

    outer_pairs = both_cores([(0, 1), (1, 0), (2, 3), (3, 2)])
    inner_pairs = both_cores([(1, 2), (2, 1)])
    acc, part, total, outer, inner, sums = {}, {}, {}, {}, {}, {}
    grams, out = None, None
    start(0, ())
    for step in range(count + 3):
        operands, shapes = {}, {}
        if step < count:
            operands["keep"], operands["swapped"] = keep[step], swapped[step]
            shapes["acc"] = sizes[step]
        if step - 1 in outer:
            operands["outer"] = outer[step - 1]
        if 0 <= step - 1 < count:
            operands["acc_before"] = acc[step - 1]
            shapes["part"] = sizes[step - 1]
        if 0 <= step - 2 < count:
            operands["part_before"], operands["inner"] = part[step - 2], inner[step - 1]
            shapes["total"] = sizes[step - 2]
        if 0 <= step - 3 < count:
            operands["total_before"] = total[step - 3]
            shapes["final"] = sizes[step - 3]
        sent = [shapes[name] for name in ("acc", "total") if name in shapes]
        if sent:
            shapes["out"] = max(sent, key=lambda shape: shape[1])
        results = exchange(ends, operands, shapes)
        if "out" in results:
            outer[step] = lax.ppermute(results["out"], "row", outer_pairs)
        if "acc" in results:
            acc[step] = results["acc"]
        if "part" in results:
            part[step - 1] = results["part"]
            inner[step] = lax.ppermute(results["part"], "row", inner_pairs)
        if "total" in results:
            total[step - 2] = results["total"]
        if step + 1 < count:
            start(step + 1, [next(iter(results.values()))])
        if "final" in results:
            done = step - 3
            own, other = results["final"], swap_cores(results["final"])
            if done == gram_chunk:
                pair = ordered((own[:, width:], other[:, width:]))
                gathered = lax.all_gather(jnp.concatenate(pair, axis=0), "col")
                grams = gathered[holders]
            sums[chunks[done]] = (own, other)
            index, block = chunks[done]
            if index == PANELS - 1:
                pieces = [piece for panel in range(PANELS) for piece in sums[panel, block]]
                highs, lows = zip(*[prepared[panel][:2] for panel in range(PANELS)])
                out = update(places, pieces, tfac, grams, highs, lows, eigvec, out, block, width)
    return out


def shards(eigvec, slots, roots, tfac):
    if lax.axis_size("col") == 4 and lax.axis_size("row") == 8:
        return shards_square(eigvec, slots[0], roots, tfac)
    columns = eigvec.shape[1]
    width = min(columns, BLOCK)
    rounds, places, panels = fetch_any(slots[0], roots)
    core = lax.axis_index("row") % 2
    places = jnp.where(core == 0, places, places.reshape(PANELS, 2)[:, ::-1].reshape(-1))
    x_high, x_low = split_array(eigvec)
    highs, lows, sums = [], [], []
    for first, second in rounds:
        keep = jnp.where(core == 0, first, second)
        send = jnp.where(core == 0, second, first)
        high, low, flipped = prepare(keep, send)
        highs.append(high)
        lows.append(low)
        sums.append([
            sum_over_rows(*products(flipped, x_high, x_low, block, width)) for block in range(columns // width)
        ])
    grams = jnp.stack([gram(panels[1], panels[0]), gram(panels[2], panels[0]), gram(panels[2], panels[1])])
    grams = lax.psum(grams, "row")
    out = None
    for block in range(columns // width):
        pieces = [piece for index in range(PANELS) for piece in sums[index][block]]
        out = update(places, pieces, tfac, grams, highs, lows, eigvec, out, block, width)
    return out


def solution(mesh):
    in_specs = (P("row", "col"), P("col", "row", None), P(), P())
    out_specs = P("row", "col")
    return jax.shard_map(shards, mesh=mesh, in_specs=in_specs, out_specs=out_specs, check_vma=False)
```

profile of v0, /device:TPU:0, one launch (start us, length us, event | category | flops | bytes accessed | tf_op | source)
XLA Modules:
  0.0 293.7 jit_solution(7470803121313530991)
XLA Ops:
  6.5 3.0 %fusion.12 = (f32[2048,128]{1,0:T(8,128)}, f32[2048,128]{1,0:T(8,128)}) fusion(f32[2048,256]{1,0:T(8,128)} %bitcast.25), kind=kLoop, calls=%fused_computation.48 | loop fusion | bytes 4194304 | tf_op jit(solution)/shard_map/slice | solution.py:231
  9.5 3.0 %collective-permute-start.4 = (f32[2048,128]{1,0:T(8,128)}, f32[2048,128]{1,0:T(8,128)S(1)}, u32[]{:S(2)}, u32[]{:S(2)}) collective-permute-start(f32[2048,128]{1,0:T(8,128)} %get-tuple-element.137), channel_id=1, source_target_pairs={{0,2},{1,3},{2,0},{3,1},{4,6},{5,7},{6,4},{7,5},{8,10},{9,11},{10,... | collective-permute-start | bytes 3145736 | tf_op jit(solution)/shard_map/ppermute | solution.py:230
  12.5 1.5 collective-permute-start.2
  14.6 11.3 %split_x.1 = (bf16[2048,2048]{1,0:T(8,128)(2,1)S(1)}, bf16[2048,2048]{1,0:T(8,128)(2,1)}) custom-call(f32[2048,2048]{1,0:T(8,128)} %refs_14_.3), custom_call_target="tpu_custom_call" | custom-call | flops 262144 | bytes 524288 | tf_op jit(solution)/shard_map/split_x/pallas_call | solution.py:49
  25.9 3.3 %copy-done = bf16[2048,2048]{1,0:T(8,128)(2,1)} copy-done((bf16[2048,2048]{1,0:T(8,128)(2,1)}, bf16[2048,2048]{1,0:T(8,128)(2,1)S(1)}, u32[]{:S(2)}) %copy-start) | copy-done | bytes 8388632
  32.8 3.8 %collective-permute-done.4 = f32[2048,128]{1,0:T(8,128)S(1)} collective-permute-done((f32[2048,128]{1,0:T(8,128)}, f32[2048,128]{1,0:T(8,128)S(1)}, u32[]{:S(2)}, u32[]{:S(2)}) %collective-permute-start.4) | collective-permute-done | bytes 1048608 | tf_op jit(solution)/shard_map/ppermute | solution.py:230
  36.7 2.2 collective-permute-done.2
  38.9 21.0 %collective-permute-done.5 = f32[2048,128]{1,0:T(8,128)} collective-permute-done((f32[2048,128]{1,0:T(8,128)}, f32[2048,128]{1,0:T(8,128)}, u32[]{:S(2)}, u32[]{:S(2)}) %collective-permute-start.5) | collective-permute-done | bytes 1048608 | tf_op jit(solution)/shard_map/ppermute | solution.py:230
  59.9 4.8 %broadcast_select_fusion = (f32[2048,128]{1,0:T(8,128)}, f32[2048,128]{1,0:T(8,128)}, f32[2048,128]{1,0:T(8,128)}, f32[2048,128]{1,0:T(8,128)}, f32[2048,128]{1,...) fusion(pred[]{:T(512)S(6)} %eq.11, f32[2048,128]{1,0:T(8,128)} %collective-permute-done.2, ...), kind=kLoop, calls=%fused_computation.13 | loop fusion | flops 3932160 | bytes 13631495 | tf_op jit(solution)/shard_map/jit(_where)/select_n | solution.py:318
  64.7 1.0 prepare_panel.5
  66.2 6.6 %products.7 = (f32[128,1024]{1,0:T(8,128)S(1)}, f32[128,1024]{1,0:T(8,128)}) custom-call(bf16[512,2048]{1,0:T(8,128)(2,1)S(1)} %get-tuple-element.64.flipped_ref, bf16[2048,2048]{1,0:T(8,128)(2,1)S(1)} %bitcast.22, bf16[2048,2048]{1,0:T(8,128)(2,1)} %get-tuple-element.66.low_ref), custom_call_target="tpu_custom_call" | custom-call | flops 50331648 | bytes 163840 | tf_op jit(solution)/shard_map/products/pallas_call | solution.py:109
  73.8 1.7 collective-permute-start.1
  75.8 1.0 copy-done.33
  76.8 1.9 exchange.9
  78.7 3.6 %copy-done.1 = bf16[2048,2048]{1,0:T(8,128)(2,1)S(1)} copy-done((bf16[2048,2048]{1,0:T(8,128)(2,1)S(1)}, bf16[2048,2048]{1,0:T(8,128)(2,1)}, u32[]{:S(2)}) %copy-start.1) | copy-done | bytes 8388632
  82.3 6.5 %products.8 = (f32[128,1024]{1,0:T(8,128)S(1)}, f32[128,1024]{1,0:T(8,128)}) custom-call(bf16[512,2048]{1,0:T(8,128)(2,1)S(1)} %get-tuple-element.64.flipped_ref, bf16[2048,2048]{1,0:T(8,128)(2,1)S(1)} %copy-done.1, bf16[2048,2048]{1,0:T(8,128)(2,1)} %get-tuple-element.66.low_ref, f32[128,1024]{1,0:T(8,128)S(1)} %get-tuple-element.69.refs_0_.refs_3_), custom_call_target="tpu_custom_call" | custom-call | flops 50331648 | bytes 163840 | tf_op jit(solution)/shard_map/products/pallas_call | solution.py:109
  89.8 1.6 collective-permute-start.8
  91.7 12.4 %collective-permute-done.8.refs_2_ = f32[128,1024]{1,0:T(8,128)S(1)} collective-permute-done((f32[128,1024]{1,0:T(8,128)}, f32[128,1024]{1,0:T(8,128)S(1)}, u32[]{:S(2)}, u32[]{:S(2)}) %collective-permute-start.8) | collective-permute-done | bytes 524320 | tf_op jit(solution)/shard_map/ppermute | solution.py:364
  104.2 1.0 copy-done.21
  105.2 1.0 copy-done.27
  106.4 1.6 collective-permute-start.10
  108.9 4.9 %broadcast_select_fusion.4 = (f32[2048,128]{1,0:T(8,128)S(1)}, f32[2048,128]{1,0:T(8,128)S(1)}, f32[2048,128]{1,0:T(8,128)S(1)}, f32[2048,128]{1,0:T(8,128)}, f32[2048,128]{1,0:T(8,128)}) fusion(pred[]{:T(512)S(6)} %eq.11, f32[2048,128]{1,0:T(8,128)} %copy-done.37, f32[2048,128]{1,0:T(8,128)} %collective-permute-done.2, ...), kind=kLoop, calls=%fused_computation.17 | loop fusion | flops 2883584 | bytes 11534340 | tf_op jit(solution)/shard_map/jit(_where)/select_n | solution.py:318
  113.9 1.0 prepare_panel.6
  115.0 6.7 %products.9 = (f32[128,1024]{1,0:T(8,128)S(1)}, f32[128,1024]{1,0:T(8,128)S(1)}) custom-call(bf16[512,2048]{1,0:T(8,128)(2,1)S(1)} %get-tuple-element.74.flipped_ref, bf16[2048,2048]{1,0:T(8,128)(2,1)S(1)} %bitcast.24, bf16[2048,2048]{1,0:T(8,128)(2,1)} %get-tuple-element.66.low_ref, f32[128,1024]{1,0:T(8,128)S(1)} %get-tuple-element.73.refs_0_.refs_3_), custom_call_target="tpu_custom_call" | custom-call | flops 50331648 | bytes 163840 | tf_op jit(solution)/shard_map/products/pallas_call | solution.py:109
  122.0 1.7 collective-permute-done.9.refs_1_
  124.8 6.0 %products.10 = (f32[128,1024]{1,0:T(8,128)S(1)}, f32[128,1024]{1,0:T(8,128)S(1)}) custom-call(bf16[512,2048]{1,0:T(8,128)(2,1)S(1)} %get-tuple-element.74.flipped_ref, bf16[2048,2048]{1,0:T(8,128)(2,1)S(1)} %bitcast.24, bf16[2048,2048]{1,0:T(8,128)(2,1)} %get-tuple-element.66.low_ref, f32[128,1024]{1,0:T(8,128)S(1)} %get-tuple-element.79.refs_0_.refs_3_), custom_call_target="tpu_custom_call" | custom-call | flops 50331648 | bytes 163840 | tf_op jit(solution)/shard_map/products/pallas_call | solution.py:109
  130.9 2.4 prepare_panel.8
  133.3 2.0 prepare_panel.7
  135.3 1.0 products.11
  136.6 4.2 %collective-permute-start.13 = (f32[128,1024]{1,0:T(8,128)S(1)}, f32[128,1024]{1,0:T(8,128)S(1)}, u32[]{:S(2)}, u32[]{:S(2)}) collective-permute-start(f32[128,1024]{1,0:T(8,128)S(1)} %copy-done.35), channel_id=1, source_target_pairs={{0,8},{4,12},{8,0},{12,4},{16,24},{20,28},{24,16},{28,20},{1,9},{5... | collective-permute-start | bytes 1572872 | tf_op jit(solution)/shard_map/ppermute | solution.py:364
  141.5 11.7 %collective-permute-done.13.refs_2_ = f32[128,1024]{1,0:T(8,128)S(1)} collective-permute-done((f32[128,1024]{1,0:T(8,128)S(1)}, f32[128,1024]{1,0:T(8,128)S(1)}, u32[]{:S(2)}, u32[]{:S(2)}) %collective-permute-start.13) | collective-permute-done | bytes 524320 | tf_op jit(solution)/shard_map/ppermute | solution.py:364
  153.2 1.1 exchange.12
  154.3 3.6 %collective-permute-start.16 = (f32[128,1280]{1,0:T(8,128)S(1)}, f32[128,1280]{1,0:T(8,128)S(1)}, u32[]{:S(2)}, u32[]{:S(2)}) collective-permute-start(f32[128,1280]{1,0:T(8,128)S(1)} %get-tuple-element.94), channel_id=1, source_target_pairs={{0,8},{4,12},{8,0},{12,4},{16,24},{20,28},{24,16},{28,20},{1,9},{5... | collective-permute-start | bytes 1966088 | tf_op jit(solution)/shard_map/ppermute | solution.py:364
  158.6 1.0 prepare_panel.9
  159.7 6.5 %products.12 = (f32[128,1024]{1,0:T(8,128)S(1)}, f32[128,1024]{1,0:T(8,128)S(1)}) custom-call(bf16[512,2048]{1,0:T(8,128)(2,1)S(1)} %get-tuple-element.91.flipped_ref, bf16[2048,2048]{1,0:T(8,128)(2,1)S(1)} %bitcast.24, bf16[2048,2048]{1,0:T(8,128)(2,1)} %get-tuple-element.66.low_ref, f32[128,1280]{1,0:T(8,128)S(1)} %get-tuple-element.90.refs_0_.refs_3_), custom_call_target="tpu_custom_call" | custom-call | flops 50331648 | bytes 163840 | tf_op jit(solution)/shard_map/products/pallas_call | solution.py:109
  166.3 1.9 collective-permute-done.15.refs_1_
  168.2 4.2 %collective-permute-done.16.refs_2_ = f32[128,1280]{1,0:T(8,128)S(1)} collective-permute-done((f32[128,1280]{1,0:T(8,128)S(1)}, f32[128,1280]{1,0:T(8,128)S(1)}, u32[]{:S(2)}, u32[]{:S(2)}) %collective-permute-start.16) | collective-permute-done | bytes 655392 | tf_op jit(solution)/shard_map/ppermute | solution.py:364
  172.4 1.1 exchange.13
  173.5 0.9 collective-permute-start.21
  174.3 3.5 %collective-permute-start.20 = (f32[128,1024]{1,0:T(8,128)S(1)}, f32[128,1024]{1,0:T(8,128)S(1)}, u32[]{:S(2)}, u32[]{:S(2)}) collective-permute-start(f32[128,1024]{1,0:T(8,128)S(1)} %get-tuple-element.101), channel_id=1, source_target_pairs={{0,8},{4,12},{8,0},{12,4},{16,24},{20,28},{24,16},{28,20},{1,9},{5... | collective-permute-start | bytes 1572872 | tf_op jit(solution)/shard_map/ppermute | solution.py:364
  177.9 5.9 %products.13 = (f32[128,1024]{1,0:T(8,128)S(1)}, f32[128,1024]{1,0:T(8,128)S(1)}) custom-call(bf16[512,2048]{1,0:T(8,128)(2,1)S(1)} %get-tuple-element.91.flipped_ref, bf16[2048,2048]{1,0:T(8,128)(2,1)S(1)} %bitcast.24, bf16[2048,2048]{1,0:T(8,128)(2,1)} %get-tuple-element.66.low_ref, f32[128,1024]{1,0:T(8,128)S(1)} %get-tuple-element.98.refs_0_.refs_3_), custom_call_target="tpu_custom_call" | custom-call | flops 50331648 | bytes 163840 | tf_op jit(solution)/shard_map/products/pallas_call | solution.py:109
  183.9 4.7 %collective-permute-done.20.refs_2_ = f32[128,1024]{1,0:T(8,128)S(1)} collective-permute-done((f32[128,1024]{1,0:T(8,128)S(1)}, f32[128,1024]{1,0:T(8,128)S(1)}, u32[]{:S(2)}, u32[]{:S(2)}) %collective-permute-start.20) | collective-permute-done | bytes 524320 | tf_op jit(solution)/shard_map/ppermute | solution.py:364
  188.6 1.1 exchange.14
  189.7 3.8 %collective-permute-start.22 = (f32[128,1280]{1,0:T(8,128)S(1)}, f32[128,1280]{1,0:T(8,128)S(1)}, u32[]{:S(2)}, u32[]{:S(2)}) collective-permute-start(f32[128,1280]{1,0:T(8,128)S(1)} %get-tuple-element.104), channel_id=1, source_target_pairs={{0,8},{4,12},{8,0},{12,4},{16,24},{20,28},{24,16},{28,20},{1,9},{5... | collective-permute-start | bytes 1966088 | tf_op jit(solution)/shard_map/ppermute | solution.py:364
  194.2 11.9 %collective-permute-done.22.refs_0_ = f32[128,1280]{1,0:T(8,128)S(1)} collective-permute-done((f32[128,1280]{1,0:T(8,128)S(1)}, f32[128,1280]{1,0:T(8,128)S(1)}, u32[]{:S(2)}, u32[]{:S(2)}) %collective-permute-start.22) | collective-permute-done | bytes 655392 | tf_op jit(solution)/shard_map/ppermute | solution.py:364
  206.1 1.0 exchange.15
  207.1 1.7 collective-permute-start.25
  209.6 0.8 copy-done.22
  210.4 0.9 copy-done.24
  212.0 9.6 %collective-permute-done.25.refs_0_ = f32[128,1024]{1,0:T(8,128)S(1)} collective-permute-done((f32[128,1024]{1,0:T(8,128)}, f32[128,1024]{1,0:T(8,128)S(1)}, u32[]{:S(2)}, u32[]{:S(2)}) %collective-permute-start.25) | collective-permute-done | bytes 524320 | tf_op jit(solution)/shard_map/ppermute | solution.py:364
  221.6 1.1 exchange.16
  222.7 0.9 copy-done.28
  223.6 3.4 %collective-permute-start.27 = (f32[128,1024]{1,0:T(8,128)}, f32[128,1024]{1,0:T(8,128)S(1)}, u32[]{:S(2)}, u32[]{:S(2)}) collective-permute-start(f32[128,1024]{1,0:T(8,128)} %get-tuple-element.112), channel_id=1, source_target_pairs={{0,8},{4,12},{8,0},{12,4},{16,24},{20,28},{24,16},{28,20},{1,9},{5... | collective-permute-start | bytes 1572872 | tf_op jit(solution)/shard_map/ppermute | solution.py:364
  228.3 10.6 %collective-permute-done.27.refs_0_ = f32[128,1024]{1,0:T(8,128)S(1)} collective-permute-done((f32[128,1024]{1,0:T(8,128)}, f32[128,1024]{1,0:T(8,128)S(1)}, u32[]{:S(2)}, u32[]{:S(2)}) %collective-permute-start.27) | collective-permute-done | bytes 524320 | tf_op jit(solution)/shard_map/ppermute | solution.py:364
  238.8 1.0 copy-done.29
  239.9 0.9 exchange.17.refs_4_
  241.1 1.8 gather_fusion
  243.0 1.2 copy-done.5
  244.2 1.2 copy-done.7
  245.4 1.2 copy-done.9
  246.6 1.2 copy-done.12
  247.9 1.1 copy-done.18
  249.0 19.2 %update.2.refs_15_ = f32[2048,2048]{1,0:T(8,128)} custom-call(s32[6]{0:T(128)S(1)} %broadcast_select_fusion.8.place_ref, f32[128,1024]{1,0:T(8,128)} %get-tuple-element.120.refs_0_, f32[128,1024]{1,0:T(8,128)} %collective-permute-done.29.refs_1_, f32[128,1024]{1,0:T(8,128)} %get-tuple-element.121.refs_2_, f32[128,1024]{1,0:T(8,128)} %collective-permute-done.30.refs_3_, ...), custom_call_target="tpu_custom_call" | custom-call | flops 150994944 | bytes 360448 | tf_op jit(solution)/shard_map/update/pallas_call | solution.py:173
  268.2 18.6 %update.3 = f32[2048,2048]{1,0:T(8,128)} custom-call(s32[6]{0:T(128)S(1)} %broadcast_select_fusion.8.place_ref, f32[128,1024]{1,0:T(8,128)} %get-tuple-element.97.refs_0_, f32[128,1024]{1,0:T(8,128)} %collective-permute-done.18.refs_1_, f32[128,1280]{1,0:T(8,128)S(1)} %copy-done.23, f32[128,1280]{1,0:T(8,128)S(1)} %copy-done.25, ...), custom_call_target="tpu_custom_call", output_to_operand_aliasing={{}: (16, {})} | custom-call | flops 150994944 | bytes 360448 | tf_op jit(solution)/shard_map/update/pallas_call | solution.py:173
  (150 shorter events, 12.7 us)
Async XLA Ops:
  6.5 234.5 %all-gather.3.cloned.1.call-start = ((), (), s32[]{:S(2)}) async-start(), calls=%async_computation | async-start | bytes 1310720 | tf_op jit(solution)/shard_map/all_gather | solution.py:379
  9.5 27.2 %collective-permute-start.4 = (f32[2048,128]{1,0:T(8,128)}, f32[2048,128]{1,0:T(8,128)S(1)}, u32[]{:S(2)}, u32[]{:S(2)}) collective-permute-start(f32[2048,128]{1,0:T(8,128)} %get-tuple-element.137), channel_id=1, source_target_pairs={{0,2},{1,3},{2,0},{3,1},{4,6},{5,7},{6,4},{7,5},{8,10},{9,11},{10,... | collective-permute-start | bytes 3145736 | tf_op jit(solution)/shard_map/ppermute | solution.py:230
  12.5 26.4 %collective-permute-start.2 = (f32[2048,128]{1,0:T(8,128)}, f32[2048,128]{1,0:T(8,128)}, u32[]{:S(2)}, u32[]{:S(2)}) collective-permute-start(f32[2048,128]{1,0:T(8,128)} %get-tuple-element.137), channel_id=1, source_target_pairs={{0,1},{1,0},{2,3},{3,2},{4,5},{5,4},{6,7},{7,6},{8,9},{9,8},{10,11... | collective-permute-start | bytes 3145736 | tf_op jit(solution)/shard_map/ppermute | solution.py:230
  14.0 15.3 %copy-start.40 = (s32[3]{0:T(128)S(1)}, s32[3]{0:T(128)}, u32[]{:S(2)}) copy-start(s32[3]{0:T(128)} %param.11) | copy-start | bytes 40
  14.0 15.4 %copy-start.44 = (s32[2,4]{1,0:T(2,128)S(1)}, s32[2,4]{1,0:T(2,128)}, u32[]{:S(2)}) copy-start(s32[2,4]{1,0:T(2,128)} %constant.81.clone) | copy-start | bytes 100
  14.0 17.2 %copy-start.43 = (s32[2,4]{1,0:T(2,128)S(1)}, s32[2,4]{1,0:T(2,128)}, u32[]{:S(2)}) copy-start(s32[2,4]{1,0:T(2,128)} %constant.80.clone) | copy-start | bytes 100
  14.0 45.9 %copy-start.36 = (f32[1,2048,256]{2,1,0:T(8,128)S(1)}, f32[1,2048,256]{2,1,0:T(8,128)}, u32[]{:S(2)}) copy-start(f32[1,2048,256]{2,1,0:T(8,128)} %param.10) | copy-start | bytes 6291460
  14.0 45.9 %collective-permute-start.5 = (f32[2048,128]{1,0:T(8,128)}, f32[2048,128]{1,0:T(8,128)}, u32[]{:S(2)}, u32[]{:S(2)}) collective-permute-start(f32[2048,128]{1,0:T(8,128)} %get-tuple-element.138), channel_id=1, source_target_pairs={{0,1},{1,0},{2,3},{3,2},{4,5},{5,4},{6,7},{7,6},{8,9},{9,8},{10,11... | collective-permute-start | bytes 3145736 | tf_op jit(solution)/shard_map/ppermute | solution.py:230
  14.6 45.3 %collective-permute-start = (f32[2048,128]{1,0:T(8,128)}, f32[2048,128]{1,0:T(8,128)}, u32[]{:S(2)}, u32[]{:S(2)}) collective-permute-start(f32[2048,128]{1,0:T(8,128)} %get-tuple-element.138), channel_id=1, source_target_pairs={{0,2},{1,3},{2,0},{3,1},{4,6},{5,7},{6,4},{7,5},{8,10},{9,11},{10,... | collective-permute-start | bytes 3145736 | tf_op jit(solution)/shard_map/ppermute | solution.py:230
  36.7 28.1 %copy-start.37 = (f32[2048,128]{1,0:T(8,128)}, f32[2048,128]{1,0:T(8,128)S(1)}, u32[]{:S(2)}) copy-start(f32[2048,128]{1,0:T(8,128)S(1)} %collective-permute-done.4) | copy-start | bytes 3145732
  59.9 5.9 %slice-start = ((s8[8388608]{0:T(1024)(128)(4,1)}), s8[4194304]{0:T(1024)(128)(4,1)S(1)}, s32[]{:S(2)}) async-start(s8[8388608]{0:T(1024)(128)(4,1)} %bitcast.21), calls=%async_computation.1 | async-start | bytes 8388608
  59.9 6.3 %slice-start.1 = ((s8[8388608]{0:T(1024)(128)(4,1)}), s8[4194304]{0:T(1024)(128)(4,1)S(1)}, s32[]{:S(2)}) async-start(s8[8388608]{0:T(1024)(128)(4,1)} %bitcast.21), calls=%async_computation.2 | async-start | bytes 8388608
  65.8 7.0 %copy-start.2 = (bf16[2048,256]{1,0:T(8,128)(2,1)}, bf16[2048,256]{1,0:T(8,128)(2,1)S(1)}, u32[]{:S(2)}) copy-start(bf16[2048,256]{1,0:T(8,128)(2,1)S(1)} %get-tuple-element.117.refs_11_) | copy-start | bytes 3145732
  73.5 2.3 collective-permute-start.6
  73.5 35.4 %collective-permute-start.3 = (f32[2048,128]{1,0:T(8,128)}, f32[2048,128]{1,0:T(8,128)}, u32[]{:S(2)}, u32[]{:S(2)}) collective-permute-start(f32[2048,128]{1,0:T(8,128)} %collective-permute-done.2), channel_id=1, source_target_pairs={{0,2},{1,3},{2,0},{3,1},{4,6},{5,7},{6,4},{7,5},{8,10},{9,11},{10,... | collective-permute-start | bytes 3145736 | tf_op jit(solution)/shard_map/ppermute | solution.py:230
  73.8 35.1 %collective-permute-start.1 = (f32[2048,128]{1,0:T(8,128)}, f32[2048,128]{1,0:T(8,128)}, u32[]{:S(2)}, u32[]{:S(2)}) collective-permute-start(f32[2048,128]{1,0:T(8,128)} %collective-permute-done), channel_id=1, source_target_pairs={{0,1},{1,0},{2,3},{3,2},{4,5},{5,4},{6,7},{7,6},{8,9},{9,8},{10,11... | collective-permute-start | bytes 3145736 | tf_op jit(solution)/shard_map/ppermute | solution.py:230
  78.7 10.1 %copy-start.20 = (f32[128,1024]{1,0:T(8,128)}, f32[128,1024]{1,0:T(8,128)S(1)}, u32[]{:S(2)}) copy-start(f32[128,1024]{1,0:T(8,128)S(1)} %get-tuple-element.69.refs_0_.refs_3_) | copy-start | bytes 1572868
  78.7 3.6 %copy-start.1 = (bf16[2048,2048]{1,0:T(8,128)(2,1)S(1)}, bf16[2048,2048]{1,0:T(8,128)(2,1)}, u32[]{:S(2)}) copy-start(bf16[2048,2048]{1,0:T(8,128)(2,1)} %copy-done) | copy-start | bytes 25165828
  89.6 2.1 collective-permute-start.7
  89.8 14.4 %collective-permute-start.8 = (f32[128,1024]{1,0:T(8,128)}, f32[128,1024]{1,0:T(8,128)S(1)}, u32[]{:S(2)}, u32[]{:S(2)}) collective-permute-start(f32[128,1024]{1,0:T(8,128)} %get-tuple-element.72), channel_id=1, source_target_pairs={{0,8},{4,12},{8,0},{12,4},{16,24},{20,28},{24,16},{28,20},{1,9},{5... | collective-permute-start | bytes 1572872 | tf_op jit(solution)/shard_map/ppermute | solution.py:364
  106.3 8.7 %slice-start.2 = ((s8[8388608]{0:T(1024)(128)(4,1)}), s8[4194304]{0:T(1024)(128)(4,1)S(1)}, s32[]{:S(2)}) async-start(s8[8388608]{0:T(1024)(128)(4,1)} %bitcast.23), calls=%async_computation.3 | async-start | bytes 8388608
  106.4 15.6 %collective-permute-start.10 = (f32[128,1024]{1,0:T(8,128)S(1)}, f32[128,1024]{1,0:T(8,128)S(1)}, u32[]{:S(2)}, u32[]{:S(2)}) collective-permute-start(f32[128,1024]{1,0:T(8,128)S(1)} %get-tuple-element.77), channel_id=1, source_target_pairs={{0,8},{4,12},{8,0},{12,4},{16,24},{20,28},{24,16},{28,20},{1,9},{5... | collective-permute-start | bytes 1572872 | tf_op jit(solution)/shard_map/ppermute | solution.py:364
  108.0 7.0 %slice-start.3 = ((s8[8388608]{0:T(1024)(128)(4,1)}), s8[4194304]{0:T(1024)(128)(4,1)S(1)}, s32[]{:S(2)}) async-start(s8[8388608]{0:T(1024)(128)(4,1)} %bitcast.23), calls=%async_computation.4 | async-start | bytes 8388608
  108.0 14.0 %collective-permute-start.11 = (f32[128,1024]{1,0:T(8,128)S(1)}, f32[128,1024]{1,0:T(8,128)S(1)}, u32[]{:S(2)}, u32[]{:S(2)}) collective-permute-start(f32[128,1024]{1,0:T(8,128)S(1)} %get-tuple-element.78.refs_4_), channel_id=1, source_target_pairs={{8,16},{12,20},{16,8},{20,12},{9,17},{13,21},{17,9},{21,13},{10,18... | collective-permute-start | bytes 1572872 | tf_op jit(solution)/shard_map/ppermute | solution.py:369
  115.0 6.8 %copy-start.4 = (bf16[2048,256]{1,0:T(8,128)(2,1)}, bf16[2048,256]{1,0:T(8,128)(2,1)S(1)}, u32[]{:S(2)}) copy-start(bf16[2048,256]{1,0:T(8,128)(2,1)S(1)} %get-tuple-element.115.refs_9_) | copy-start | bytes 3145732
  115.0 6.8 %copy-start.6 = (bf16[2048,256]{1,0:T(8,128)(2,1)}, bf16[2048,256]{1,0:T(8,128)(2,1)S(1)}, u32[]{:S(2)}) copy-start(bf16[2048,256]{1,0:T(8,128)(2,1)S(1)} %get-tuple-element.118.refs_12_) | copy-start | bytes 3145732
  115.0 6.9 %copy-start.38 = (f32[2048,128]{1,0:T(8,128)S(1)}, f32[2048,128]{1,0:T(8,128)}, u32[]{:S(2)}) copy-start(f32[2048,128]{1,0:T(8,128)} %get-tuple-element.127) | copy-start | bytes 3145732
  115.0 6.9 %copy-start.39 = (f32[2048,128]{1,0:T(8,128)S(1)}, f32[2048,128]{1,0:T(8,128)}, u32[]{:S(2)}) copy-start(f32[2048,128]{1,0:T(8,128)} %get-tuple-element.128) | copy-start | bytes 3145732
  121.8 2.0 collective-permute-start.9
  124.8 6.1 %copy-start.14 = (f32[2048,128]{1,0:T(8,128)S(1)}, f32[2048,128]{1,0:T(8,128)}, u32[]{:S(2)}) copy-start(f32[2048,128]{1,0:T(8,128)} %get-tuple-element.129.send_ref) | copy-start | bytes 3145732
  124.8 6.1 %copy-start.15 = (f32[2048,128]{1,0:T(8,128)S(1)}, f32[2048,128]{1,0:T(8,128)}, u32[]{:S(2)}) copy-start(f32[2048,128]{1,0:T(8,128)} %get-tuple-element.131.keep_ref) | copy-start | bytes 3145732
  135.3 6.1 %copy-start.31 = (f32[128,1024]{1,0:T(8,128)S(1)}, f32[128,1024]{1,0:T(8,128)}, u32[]{:S(2)}) copy-start(f32[128,1024]{1,0:T(8,128)} %copy-done.30) | copy-start | bytes 1572868
  136.4 16.8 %collective-permute-start.12 = (f32[128,1280]{1,0:T(8,128)S(1)}, f32[128,1280]{1,0:T(8,128)S(1)}, u32[]{:S(2)}, u32[]{:S(2)}) collective-permute-start(f32[128,1280]{1,0:T(8,128)S(1)} %pad_maximum_fusion.1), channel_id=1, source_target_pairs={{0,4},{4,0},{8,12},{12,8},{16,20},{20,16},{24,28},{28,24},{1,5},{5... | collective-permute-start | bytes 1966088 | tf_op jit(solution)/shard_map/ppermute | solution.py:200
  136.6 16.6 %collective-permute-start.13 = (f32[128,1024]{1,0:T(8,128)S(1)}, f32[128,1024]{1,0:T(8,128)S(1)}, u32[]{:S(2)}, u32[]{:S(2)}) collective-permute-start(f32[128,1024]{1,0:T(8,128)S(1)} %copy-done.35), channel_id=1, source_target_pairs={{0,8},{4,12},{8,0},{12,4},{16,24},{20,28},{24,16},{28,20},{1,9},{5... | collective-permute-start | bytes 1572872 | tf_op jit(solution)/shard_map/ppermute | solution.py:364
  140.8 12.5 %collective-permute-start.14 = (f32[128,1024]{1,0:T(8,128)S(1)}, f32[128,1024]{1,0:T(8,128)S(1)}, u32[]{:S(2)}, u32[]{:S(2)}) collective-permute-start(f32[128,1024]{1,0:T(8,128)S(1)} %get-tuple-element.88.refs_4_), channel_id=1, source_target_pairs={{8,16},{12,20},{16,8},{20,12},{9,17},{13,21},{17,9},{21,13},{10,18... | collective-permute-start | bytes 1572872 | tf_op jit(solution)/shard_map/ppermute | solution.py:369
  141.5 17.1 %copy-start.16 = (f32[2048,128]{1,0:T(8,128)S(1)}, f32[2048,128]{1,0:T(8,128)}, u32[]{:S(2)}) copy-start(f32[2048,128]{1,0:T(8,128)} %get-tuple-element.135.keep_ref) | copy-start | bytes 3145732
  141.5 17.1 %copy-start.17 = (f32[2048,128]{1,0:T(8,128)S(1)}, f32[2048,128]{1,0:T(8,128)}, u32[]{:S(2)}) copy-start(f32[2048,128]{1,0:T(8,128)} %get-tuple-element.136.send_ref) | copy-start | bytes 3145732
  154.3 18.1 %collective-permute-start.16 = (f32[128,1280]{1,0:T(8,128)S(1)}, f32[128,1280]{1,0:T(8,128)S(1)}, u32[]{:S(2)}, u32[]{:S(2)}) collective-permute-start(f32[128,1280]{1,0:T(8,128)S(1)} %get-tuple-element.94), channel_id=1, source_target_pairs={{0,8},{4,12},{8,0},{12,4},{16,24},{20,28},{24,16},{28,20},{1,9},{5... | collective-permute-start | bytes 1966088 | tf_op jit(solution)/shard_map/ppermute | solution.py:364
  157.9 8.4 %collective-permute-start.17 = (f32[128,1024]{1,0:T(8,128)S(1)}, f32[128,1024]{1,0:T(8,128)S(1)}, u32[]{:S(2)}, u32[]{:S(2)}) collective-permute-start(f32[128,1024]{1,0:T(8,128)S(1)} %get-tuple-element.95.refs_4_), channel_id=1, source_target_pairs={{8,16},{12,20},{16,8},{20,12},{9,17},{13,21},{17,9},{21,13},{10,18... | collective-permute-start | bytes 1572872 | tf_op jit(solution)/shard_map/ppermute | solution.py:369
  159.7 6.5 %copy-start.8 = (bf16[2048,256]{1,0:T(8,128)(2,1)}, bf16[2048,256]{1,0:T(8,128)(2,1)S(1)}, u32[]{:S(2)}) copy-start(bf16[2048,256]{1,0:T(8,128)(2,1)S(1)} %get-tuple-element.116.refs_10_) | copy-start | bytes 3145732
  159.7 6.5 %copy-start.11 = (bf16[2048,256]{1,0:T(8,128)(2,1)}, bf16[2048,256]{1,0:T(8,128)(2,1)S(1)}, u32[]{:S(2)}) copy-start(bf16[2048,256]{1,0:T(8,128)(2,1)S(1)} %get-tuple-element.119.refs_13_) | copy-start | bytes 3145732
  166.2 2.0 collective-permute-start.15
  173.5 15.1 %collective-permute-start.21 = (f32[128,1280]{1,0:T(8,128)S(1)}, f32[128,1280]{1,0:T(8,128)S(1)}, u32[]{:S(2)}, u32[]{:S(2)}) collective-permute-start(f32[128,1280]{1,0:T(8,128)S(1)} %get-tuple-element.102.refs_4_), channel_id=1, source_target_pairs={{8,16},{12,20},{16,8},{20,12},{9,17},{13,21},{17,9},{21,13},{10,18... | collective-permute-start | bytes 1966088 | tf_op jit(solution)/shard_map/ppermute | solution.py:369
  174.3 14.2 %collective-permute-start.20 = (f32[128,1024]{1,0:T(8,128)S(1)}, f32[128,1024]{1,0:T(8,128)S(1)}, u32[]{:S(2)}, u32[]{:S(2)}) collective-permute-start(f32[128,1024]{1,0:T(8,128)S(1)} %get-tuple-element.101), channel_id=1, source_target_pairs={{0,8},{4,12},{8,0},{12,4},{16,24},{20,28},{24,16},{28,20},{1,9},{5... | collective-permute-start | bytes 1572872 | tf_op jit(solution)/shard_map/ppermute | solution.py:364
  183.8 4.8 %collective-permute-start.19 = (f32[128,1024]{1,0:T(8,128)S(1)}, f32[128,1024]{1,0:T(8,128)S(1)}, u32[]{:S(2)}, u32[]{:S(2)}) collective-permute-start(f32[128,1024]{1,0:T(8,128)S(1)} %get-tuple-element.100), channel_id=1, source_target_pairs={{0,4},{4,0},{8,12},{12,8},{16,20},{20,16},{24,28},{28,24},{1,5},{5... | collective-permute-start | bytes 1572872 | tf_op jit(solution)/shard_map/ppermute | solution.py:200
  189.7 16.4 %collective-permute-start.22 = (f32[128,1280]{1,0:T(8,128)S(1)}, f32[128,1280]{1,0:T(8,128)S(1)}, u32[]{:S(2)}, u32[]{:S(2)}) collective-permute-start(f32[128,1280]{1,0:T(8,128)S(1)} %get-tuple-element.104), channel_id=1, source_target_pairs={{0,8},{4,12},{8,0},{12,4},{16,24},{20,28},{24,16},{28,20},{1,9},{5... | collective-permute-start | bytes 1966088 | tf_op jit(solution)/shard_map/ppermute | solution.py:364
  193.5 0.7 collective-permute-start.23
  207.1 19.9 %copy-start.41 = (s32[4,6]{1,0:T(4,128)S(1)}, s32[4,6]{1,0:T(4,128)}, u32[]{:S(2)}) copy-start(s32[4,6]{1,0:T(4,128)} %constant.79.clone) | copy-start | bytes 292
  207.1 19.9 %copy-start.42 = (s32[4,6]{1,0:T(4,128)S(1)}, s32[4,6]{1,0:T(4,128)}, u32[]{:S(2)}) copy-start(s32[4,6]{1,0:T(4,128)} %constant.78.clone) | copy-start | bytes 292
  207.1 2.4 collective-permute-start.24
  207.1 14.5 %collective-permute-start.25 = (f32[128,1024]{1,0:T(8,128)}, f32[128,1024]{1,0:T(8,128)S(1)}, u32[]{:S(2)}, u32[]{:S(2)}) collective-permute-start(f32[128,1024]{1,0:T(8,128)} %get-tuple-element.109), channel_id=1, source_target_pairs={{0,8},{4,12},{8,0},{12,4},{16,24},{20,28},{24,16},{28,20},{1,9},{5... | collective-permute-start | bytes 1572872 | tf_op jit(solution)/shard_map/ppermute | solution.py:364
  208.8 12.8 %collective-permute-start.26 = (f32[128,1024]{1,0:T(8,128)S(1)}, f32[128,1024]{1,0:T(8,128)S(1)}, u32[]{:S(2)}, u32[]{:S(2)}) collective-permute-start(f32[128,1024]{1,0:T(8,128)S(1)} %get-tuple-element.110.refs_1_), channel_id=1, source_target_pairs={{8,16},{12,20},{16,8},{20,12},{9,17},{13,21},{17,9},{21,13},{10,18... | collective-permute-start | bytes 1572872 | tf_op jit(solution)/shard_map/ppermute | solution.py:369
  212.0 29.0 %copy-start.45 = (s32[2,3]{1,0:T(2,128)S(1)}, s32[2,3]{1,0:T(2,128)}, u32[]{:S(2)}) copy-start(s32[2,3]{1,0:T(2,128)} %constant.82.clone) | copy-start | bytes 76
  223.6 19.3 %copy-start.3 = (bf16[2048,256]{1,0:T(8,128)(2,1)S(1)}, bf16[2048,256]{1,0:T(8,128)(2,1)}, u32[]{:S(2)}) copy-start(bf16[2048,256]{1,0:T(8,128)(2,1)} %copy-done.2) | copy-start | bytes 3145732
  223.6 15.2 %collective-permute-start.27 = (f32[128,1024]{1,0:T(8,128)}, f32[128,1024]{1,0:T(8,128)S(1)}, u32[]{:S(2)}, u32[]{:S(2)}) collective-permute-start(f32[128,1024]{1,0:T(8,128)} %get-tuple-element.112), channel_id=1, source_target_pairs={{0,8},{4,12},{8,0},{12,4},{16,24},{20,28},{24,16},{28,20},{1,9},{5... | collective-permute-start | bytes 1572872 | tf_op jit(solution)/shard_map/ppermute | solution.py:364
  227.2 15.7 %collective-permute-start.29 = (f32[128,1024]{1,0:T(8,128)}, f32[128,1024]{1,0:T(8,128)}, u32[]{:S(2)}, u32[]{:S(2)}) collective-permute-start(f32[128,1024]{1,0:T(8,128)} %get-tuple-element.120.refs_0_), channel_id=1, source_target_pairs={{0,4},{4,0},{8,12},{12,8},{16,20},{20,16},{24,28},{28,24},{1,5},{5... | collective-permute-start | bytes 1572872 | tf_op jit(solution)/shard_map/ppermute | solution.py:200
  227.2 40.9 %collective-permute-start.18 = (f32[128,1024]{1,0:T(8,128)}, f32[128,1024]{1,0:T(8,128)}, u32[]{:S(2)}, u32[]{:S(2)}) collective-permute-start(f32[128,1024]{1,0:T(8,128)} %get-tuple-element.97.refs_0_), channel_id=1, source_target_pairs={{0,4},{4,0},{8,12},{12,8},{16,20},{20,16},{24,28},{28,24},{1,5},{5... | collective-permute-start | bytes 1572872 | tf_op jit(solution)/shard_map/ppermute | solution.py:200
  227.8 15.2 %collective-permute-start.30 = (f32[128,1024]{1,0:T(8,128)}, f32[128,1024]{1,0:T(8,128)}, u32[]{:S(2)}, u32[]{:S(2)}) collective-permute-start(f32[128,1024]{1,0:T(8,128)} %get-tuple-element.121.refs_2_), channel_id=1, source_target_pairs={{0,4},{4,0},{8,12},{12,8},{16,20},{20,16},{24,28},{28,24},{1,5},{5... | collective-permute-start | bytes 1572872 | tf_op jit(solution)/shard_map/ppermute | solution.py:200
  227.8 15.1 %collective-permute-start.31 = (f32[128,1024]{1,0:T(8,128)}, f32[128,1024]{1,0:T(8,128)}, u32[]{:S(2)}, u32[]{:S(2)}) collective-permute-start(f32[128,1024]{1,0:T(8,128)} %get-tuple-element.122.refs_4_), channel_id=1, source_target_pairs={{0,4},{4,0},{8,12},{12,8},{16,20},{20,16},{24,28},{28,24},{1,5},{5... | collective-permute-start | bytes 1572872 | tf_op jit(solution)/shard_map/ppermute | solution.py:200
  240.8 27.4 %collective-permute-start.28 = (f32[128,1024]{1,0:T(8,128)}, f32[128,1024]{1,0:T(8,128)}, u32[]{:S(2)}, u32[]{:S(2)}) collective-permute-start(f32[128,1024]{1,0:T(8,128)} %exchange.17.refs_4_), channel_id=1, source_target_pairs={{0,4},{4,0},{8,12},{12,8},{16,20},{20,16},{24,28},{28,24},{1,5},{5... | collective-permute-start | bytes 1572872 | tf_op jit(solution)/shard_map/ppermute | solution.py:200
  249.0 19.2 %copy-start.10 = (bf16[2048,256]{1,0:T(8,128)(2,1)S(1)}, bf16[2048,256]{1,0:T(8,128)(2,1)}, u32[]{:S(2)}) copy-start(bf16[2048,256]{1,0:T(8,128)(2,1)} %copy-done.8) | copy-start | bytes 3145732
  249.0 19.2 %copy-start.19 = (f32[3,256,256]{2,1,0:T(8,128)S(1)}, f32[3,256,256]{2,1,0:T(8,128)}, u32[]{:S(2)}) copy-start(f32[3,256,256]{2,1,0:T(8,128)} %refs_6_.3) | copy-start | bytes 2359300
  249.0 19.2 %copy-start.23 = (f32[128,1280]{1,0:T(8,128)S(1)}, f32[128,1280]{1,0:T(8,128)}, u32[]{:S(2)}) copy-start(f32[128,1280]{1,0:T(8,128)} %copy-done.22) | copy-start | bytes 1966084
  249.0 19.2 %copy-start.25 = (f32[128,1280]{1,0:T(8,128)S(1)}, f32[128,1280]{1,0:T(8,128)}, u32[]{:S(2)}) copy-start(f32[128,1280]{1,0:T(8,128)} %copy-done.24) | copy-start | bytes 1966084
  (19 other events, 24.6 us)
Sparse Core Ops, SparseCore 0:
  212.1 26.2 all-gather.2
where the time goes:
time: 295 us; the launch traced here: 294 us
  Pallas kernels  104 us (35%)
  waiting for transfers between devices  96.5 us (33%)
  starting transfers between devices  36.6 us (12%)
  local copies, waits for them, and re-layouts  28.8 us (10%)
  between operations  16.4 us (6%)
  other arithmetic  11 us (4%)
    ppermute x8, waiting for transfers between devices, shards_square(): outer[step] = lax.ppermute(results['out'], 'row', outer_pairs)  65.1 us
    pallas_call x7, Pallas kernels, products(): pl.pallas_call(products_kernel, grid=(steps,), in_specs=[pl.BlockSpec((4...  39.3 us
    pallas_call x2, Pallas kernels, update(): pl.pallas_call(update_kernel, grid_spec=pltpu.PrefetchScalarGridSpec(num_...  37.8 us
    ppermute x6, waiting for transfers between devices, fetch_square(): along = lambda value, step: lax.ppermute(value, 'col', pairs_of(4, step))  27 us
    ppermute x8, starting transfers between devices, shards_square(): outer[step] = lax.ppermute(results['out'], 'row', outer_pairs)  23.5 us
    unnamed x100, local copies, waits for them, and re-layouts  22.5 us
    pallas_call x1, Pallas kernels, split_array(): pl.pallas_call(split_kernel, grid=(rows // step,), in_specs=[spec], out_s...  11.3 us
    select_n x2, other arithmetic, shards_square(): jnp.where(core == 0, *pair[::-1])  9.77 us
  transfers between devices with their start and end apart: 33, of which 14 were waited for; matrix products, arithmetic and copies ran while one was open for 3% of the time, Pallas kernels for 21%

commit v1 on v0

--- a/solution.py
+++ b/solution.py
@@ -9,7 +9,9 @@
 
 PANELS = 3
 BLOCK = 512
-VMEM = 40 * 1024 * 1024
+LAG = 1
+PIECE = 512
+VMEM = 54 * 1024 * 1024
 F32 = jnp.float32
 BF16 = jnp.bfloat16
 ANYWHERE = pl.BlockSpec(memory_space=pl.ANY)
@@ -87,6 +89,50 @@
         cost_estimate=cost(rows * half * 8, rows * half * 24),
         name="prepare_panel",
     )(keep, send, *after)
+
+
+def choose_kernel(outputs, count, which_ref, *refs):
+    cases, outs, (panel_ref, sem) = refs[:count], refs[-2 - len(outputs) : -2], refs[-2:]
+    half = cases[0].shape[1]
+    for side in range(2):
+        for index, case in enumerate(cases):
+
+            @pl.when(which_ref[side] == index)
+            def _(case=case, side=side):
+                copy = pltpu.make_async_copy(case, panel_ref.at[:, side * half : (side + 1) * half], sem)
+                copy.start()
+                copy.wait()
+
+    use = dict(zip(outputs, outs))
+    rows, width = panel_ref.shape
+    step = min(rows, 256)
+    for start in range(0, rows, step):
+        here = slice(start, start + step)
+        value = panel_ref[here, :]
+        high, low = split(value)
+        if "high" in use:
+            use["high"][here, :] = high
+            use["low"][here, :] = low
+        if "flipped" in use:
+            high, low = split(value.T)
+            use["flipped"][:width, here] = high
+            use["flipped"][width:, here] = low
+
+
+def choose(cases, which, outputs, after=()):
+    rows, half = cases[0].shape
+    shapes = {"high": (rows, 2 * half), "low": (rows, 2 * half), "flipped": (4 * half, rows)}
+    in_vmem = pl.BlockSpec(memory_space=pltpu.VMEM)
+    return pl.pallas_call(
+        functools.partial(choose_kernel, outputs, len(cases)),
+        in_specs=[pl.BlockSpec(memory_space=pltpu.SMEM)] + [ANYWHERE] * (len(cases) + len(after)),
+        out_specs=[in_vmem] * len(outputs),
+        out_shape=[jax.ShapeDtypeStruct(shapes[name], BF16) for name in outputs],
+        scratch_shapes=[pltpu.VMEM((rows, 2 * half), F32), pltpu.SemaphoreType.DMA],
+        compiler_params=params(),
+        cost_estimate=cost(rows * half * 8, rows * half * 24),
+        name="choose_panel",
+    )(which, *cases, *after)
 
 
 def products_kernel(flipped_ref, high_ref, low_ref, *refs):
@@ -237,9 +283,9 @@
     spare = (roots[0] + 3) % 4
     case = me ^ spare
     rounds = [
-        (pick(case, near[0], own[0], own[0], own[0]), pick(case, far[0], own[1], own[1], own[1])),
-        (pick(case, near[1], far[0], near[0], near[0]), pick(case, far[1], far[1], near[1], far[0])),
-        (pick(case, cross[0], cross[0], cross[0], near[1]), pick(case, cross[1], cross[1], cross[1], far[1])),
+        ((*own, near[0], far[0]), jnp.array([[2, 3], [0, 1], [0, 1], [0, 1]], jnp.int32)[case]),
+        ((*near, *far), jnp.array([[1, 3], [2, 3], [0, 1], [0, 2]], jnp.int32)[case]),
+        ((*cross, near[1], far[1]), jnp.array([[0, 1], [0, 1], [0, 1], [2, 3]], jnp.int32)[case]),
     ]
     slots = jnp.array([[1, 2, 1, 2, 3, 3], [0, 0, 2, 2, 3, 3], [0, 0, 1, 1, 3, 3], [0, 0, 1, 2, 1, 2]], jnp.int32)
     halves = jnp.array([[0, 0, 1, 1, 0, 1], [0, 1, 0, 1, 0, 1], [0, 1, 0, 1, 0, 1], [0, 1, 0, 0, 1, 1]], jnp.int32)
@@ -247,8 +293,9 @@
     places = panel * 2 + halves[case]
     later_of = jnp.array([[0, 1, 0, 0], [1, 0, 2, 2]], jnp.int32)[roots[0] - 2, me]
     earlier_of = jnp.array([[2, 2, 0, 1], [0, 0, 1, 0]], jnp.int32)[roots[0] - 2, me]
-    later = [pick(later_of, own[h], near[h], far[h]) for h in range(2)]
-    earlier = [pick(earlier_of, own[h], near[h], far[h]) for h in range(2)]
+    both = jnp.arange(2, dtype=jnp.int32)
+    later = ((*own, *near, *far), 2 * later_of + both)
+    earlier = ((*own, *near, *far), 2 * earlier_of + both)
     holders = jnp.array([[3, 0, 1], [2, 3, 0]], jnp.int32)[roots[0] - 2]
     return rounds, places, later, earlier, holders
 
@@ -267,12 +314,16 @@
     )
 
 
-def exchange_kernel(step, ends_ref, *refs):
-    names, refs = step, list(refs)
+def exchange_kernel(names, pieces, ends_ref, *refs):
     use = dict(zip(names, refs))
     end = ends_ref[0] == 1
     if "acc" in use:
-        use["acc"][...] = use["keep"][...] + use["swapped"][...]
+        start = 0
+        for index in range(pieces):
+            keep, swapped = use["keep", index], use["swapped", index]
+            columns = slice(start, start + keep.shape[1])
+            use["acc"][:, columns] = keep[...] + swapped[...]
+            start = columns.stop
     if "part" in use:
         columns = use["part"].shape[1]
         use["part"][...] = use["acc_before"][...] + use["outer"][:, :columns]
@@ -293,18 +344,20 @@
                     use["out"][:, both:] = source[:, both:]
 
 
-def exchange(ends, operands, shapes):
-    names = list(operands) + list(shapes)
+def exchange(ends, operands, shapes, after):
+    names = list(operands) + [None] * len(after) + list(shapes)
+    pieces = sum(name[0] == "keep" for name in operands)
     in_vmem = pl.BlockSpec(memory_space=pltpu.VMEM)
     results = pl.pallas_call(
-        functools.partial(exchange_kernel, names),
-        in_specs=[pl.BlockSpec(memory_space=pltpu.SMEM)] + [in_vmem] * len(operands),
+        functools.partial(exchange_kernel, names, pieces),
+        in_specs=[pl.BlockSpec(memory_space=pltpu.SMEM)] + [in_vmem] * len(operands)
+        + [ANYWHERE] * len(after),
         out_specs=[in_vmem] * len(shapes),
         out_shape=[jax.ShapeDtypeStruct(shape, F32) for shape in shapes.values()],
         compiler_params=params(),
         cost_estimate=cost(0, 0),
         name="exchange",
-    )(ends, *operands.values())
+    )(ends, *operands.values(), *after)
     return dict(zip(shapes, results))
 
 
@@ -315,69 +368,81 @@
     chip, core = lax.axis_index("row") // 2, lax.axis_index("row") % 2
     ends = jnp.where((chip == 0) | (chip == 3), 1, 0).astype(jnp.int32).reshape(1)
     places = jnp.where(core == 0, places, places.reshape(PANELS, 2)[:, ::-1].reshape(-1))
-    ordered = lambda pair: (jnp.where(core == 0, *pair), jnp.where(core == 0, *pair[::-1]))
+    ordered = lambda pair: jnp.where(core == 0, pair, pair[::-1])
     x_high, x_low = split_array(eigvec)
     chunks = [(index, block) for index in range(PANELS) for block in range(columns // width)]
     count = len(chunks)
     gram_chunk = 3
-    prepared, keep, swapped, sizes = {}, {}, {}, {}
+    prepared, arrived, sizes, gram_pieces = {}, {}, {}, []
+    half = slot.shape[1] // 2
 
     def start(number, after):
         index, block = chunks[number]
+        pieces = []
         if index not in prepared:
-            prepared[index] = prepare(*ordered(rounds[index]), after)
-        mine, other = products(prepared[index][2], x_high, x_low, block, width, after)
+            cases, which = rounds[index]
+            prepared[index] = choose(cases, ordered(which), ("high", "low", "flipped"), after)
+        for part in range(width // PIECE):
+            pieces.append(products(prepared[index][2], x_high, x_low, block * (width // PIECE) + part, PIECE, after))
+        if number == gram_chunk - 1:
+            (flipped,) = choose(later[0], ordered(later[1]), ("flipped",), after)
+            high, low = choose(*earlier, ("high", "low"), after)
+            gram_pieces.append(products(flipped, high, low, 0, high.shape[1]))
         if number == gram_chunk:
-            flipped = prepare(*ordered(later), after)[2]
-            high, low, _ = prepare(*earlier, after)
-            extra = products(flipped, high, low, 0, high.shape[1])
-            mine = jnp.concatenate([mine, extra[0]], axis=1)
-            other = jnp.concatenate([other, extra[1]], axis=1)
-        keep[number], swapped[number], sizes[number] = mine, swap_cores(other), mine.shape
+            pieces.extend(gram_pieces)
+        arrived[number] = [(mine, swap_cores(other)) for mine, other in pieces]
+        sizes[number] = (half, sum(mine.shape[1] for mine, other in pieces))
 
     outer_pairs = both_cores([(0, 1), (1, 0), (2, 3), (3, 2)])
     inner_pairs = both_cores([(1, 2), (2, 1)])
     acc, part, total, outer, inner, sums = {}, {}, {}, {}, {}, {}
     grams, out = None, None
     start(0, ())
-    for step in range(count + 3):
+    for step in range(count + 3 * LAG):
         operands, shapes = {}, {}
+        inward, middle, outward = step - LAG, step - 2 * LAG, step - 3 * LAG
         if step < count:
-            operands["keep"], operands["swapped"] = keep[step], swapped[step]
+            for number, (mine, other) in enumerate(arrived[step]):
+                operands["keep", number], operands["swapped", number] = mine, other
             shapes["acc"] = sizes[step]
-        if step - 1 in outer:
-            operands["outer"] = outer[step - 1]
-        if 0 <= step - 1 < count:
-            operands["acc_before"] = acc[step - 1]
-            shapes["part"] = sizes[step - 1]
-        if 0 <= step - 2 < count:
-            operands["part_before"], operands["inner"] = part[step - 2], inner[step - 1]
-            shapes["total"] = sizes[step - 2]
-        if 0 <= step - 3 < count:
-            operands["total_before"] = total[step - 3]
-            shapes["final"] = sizes[step - 3]
+        if step - LAG in outer:
+            operands["outer"] = outer[step - LAG]
+        if 0 <= inward < count:
+            operands["acc_before"] = acc[inward]
+            shapes["part"] = sizes[inward]
+        if 0 <= middle < count:
+            operands["part_before"], operands["inner"] = part[middle], inner[step - LAG]
+            shapes["total"] = sizes[middle]
+        if 0 <= outward < count:
+            operands["total_before"] = total[outward]
+            shapes["final"] = sizes[outward]
         sent = [shapes[name] for name in ("acc", "total") if name in shapes]
         if sent:
             shapes["out"] = max(sent, key=lambda shape: shape[1])
-        results = exchange(ends, operands, shapes)
+        ahead = [] if out is None else [out]
+        if step == gram_chunk - 1:
+            ahead.append(gram_pieces[0][0])
+        results = exchange(ends, operands, shapes, ahead)
         if "out" in results:
             outer[step] = lax.ppermute(results["out"], "row", outer_pairs)
         if "acc" in results:
             acc[step] = results["acc"]
         if "part" in results:
-            part[step - 1] = results["part"]
+            part[inward] = results["part"]
             inner[step] = lax.ppermute(results["part"], "row", inner_pairs)
         if "total" in results:
-            total[step - 2] = results["total"]
+            total[middle] = results["total"]
         if step + 1 < count:
             start(step + 1, [next(iter(results.values()))])
         if "final" in results:
-            done = step - 3
+            done = outward
             own, other = results["final"], swap_cores(results["final"])
             if done == gram_chunk:
-                pair = ordered((own[:, width:], other[:, width:]))
-                gathered = lax.all_gather(jnp.concatenate(pair, axis=0), "col")
-                grams = gathered[holders]
+                pair = own[:, width:], other[:, width:]
+                block = jnp.where(core == 0, jnp.concatenate(pair, axis=0), jnp.concatenate(pair[::-1], axis=0))
+                spread = [block] + [lax.ppermute(block, "col", pairs_of(4, shift)) for shift in range(1, 4)]
+                places_of = holders ^ lax.axis_index("col")
+                grams = jnp.stack([pick(places_of[number], *spread) for number in range(PANELS)])
             sums[chunks[done]] = (own, other)
             index, block = chunks[done]
             if index == PANELS - 1:

time: 295 us -> 297 us (level)
  Pallas kernels: 104 us -> 174 us
  waiting for transfers between devices: 96.5 us -> 45.4 us
  local copies, waits for them, and re-layouts: 28.8 us -> 18.7 us
  between operations: 16.4 us -> 7.71 us
  starting transfers between devices: 36.6 us -> 43 us
  other arithmetic: 11 us -> 7.66 us
    pallas_call x14, Pallas kernels: 16 us -> 54.3 us  [the longest x9 27.4 us: exchange(): pl.pallas_call(functools.partial(exchange_kernel, names, pieces), in_spec...]
    ppermute x8, waiting for transfers between devices: 65.1 us -> 27.1 us  [shards_square(): outer[step] = lax.ppermute(results['out'], 'row', outer_pairs)]
    pallas_call x7 -> x13, Pallas kernels: 39.3 us -> 64.5 us  [products(): pl.pallas_call(products_kernel, grid=(steps,), in_specs=[pl.BlockSpec((4...]
    ppermute x6, waiting for transfers between devices: 27 us -> 9.54 us  [fetch_square(): along = lambda value, step: lax.ppermute(value, 'col', pairs_of(4, step))]
    unnamed x100 -> x92, local copies, waits for them, and re-layouts: 22.5 us -> 12.1 us
    select_n x6 -> x5, other arithmetic: 10 us -> 2.23 us  [the longest x4 2.21 us: shards_square(): ordered = lambda pair: jnp.where(core == 0, pair, pair[::-1])]
    ppermute x12 -> x19, waiting for transfers between devices: 4.28 us -> 8.81 us  [swap_cores(): return lax.ppermute(value, 'row', pairs_of(lax.axis_size('row'), 1))]
    ppermute x0 -> x3, starting transfers between devices: none -> 3.55 us  [shards_square(): lax.ppermute(block, 'col', pairs_of(4, shift))]
  transfers between devices with their start and end apart: 33 -> 42, of which waited for: 14 -> 13; matrix products, arithmetic and copies ran while one was open for 3% -> 4% of each run, Pallas kernels for 21% -> 48%
where the time goes in v1:
time: 297 us; the launch traced here: 296 us
  Pallas kernels  174 us (59%)
  waiting for transfers between devices  45.4 us (15%)
  starting transfers between devices  43 us (14%)
  local copies, waits for them, and re-layouts  18.7 us (6%)
  between operations  7.71 us (3%)
  other arithmetic  7.66 us (3%)
    pallas_call x13, Pallas kernels, products(): pl.pallas_call(products_kernel, grid=(steps,), in_specs=[pl.BlockSpec((4...  64.5 us
    pallas_call x2, Pallas kernels, update(): pl.pallas_call(update_kernel, grid_spec=pltpu.PrefetchScalarGridSpec(num_...  40.9 us
    pallas_call x9, Pallas kernels, exchange(): pl.pallas_call(functools.partial(exchange_kernel, names, pieces), in_spec...  27.4 us
    ppermute x8, waiting for transfers between devices, shards_square(): outer[step] = lax.ppermute(results['out'], 'row', outer_pairs)  27.1 us
    pallas_call x5, Pallas kernels, choose(): pl.pallas_call(functools.partial(choose_kernel, outputs, len(cases)), in_...  26.9 us
    ppermute x8, starting transfers between devices, shards_square(): outer[step] = lax.ppermute(results['out'], 'row', outer_pairs)  21.9 us
    pallas_call x1, Pallas kernels, split_array(): pl.pallas_call(split_kernel, grid=(rows // step,), in_specs=[spec], out_s...  14 us
    unnamed x92, local copies, waits for them, and re-layouts  12.1 us
  transfers between devices with their start and end apart: 42, of which 13 were waited for; matrix products, arithmetic and copies ran while one was open for 4% of the time, Pallas kernels for 48%

profile of v1, /device:TPU:0, one launch (start us, length us, event | category | flops | bytes accessed | tf_op | source)
XLA Modules:
  0.0 296.1 jit_solution(16793401933545247044)
XLA Ops:
  0.0 3.1 %fusion.14 = (f32[2048,128]{1,0:T(8,128)}, f32[2048,128]{1,0:T(8,128)}) fusion(f32[2048,256]{1,0:T(8,128)} %bitcast.37), kind=kLoop, calls=%fused_computation.37 | loop fusion | bytes 4194304 | tf_op jit(solution)/shard_map/slice | solution.py:277
  3.1 2.9 collective-permute-start.5
  6.0 1.5 collective-permute-start
  8.8 14.0 %split_x.1 = (bf16[2048,2048]{1,0:T(8,128)(2,1)}, bf16[2048,2048]{1,0:T(8,128)(2,1)}) custom-call(f32[2048,2048]{1,0:T(8,128)} %refs_14_.3), custom_call_target="tpu_custom_call" | custom-call | flops 262144 | bytes 524288 | tf_op jit(solution)/shard_map/split_x/pallas_call | solution.py:51
  22.8 7.5 %collective-permute-done.5.refs_2_.refs_0_ = f32[2048,128]{1,0:T(8,128)} collective-permute-done((f32[2048,128]{1,0:T(8,128)}, f32[2048,128]{1,0:T(8,128)}, u32[]{:S(2)}, u32[]{:S(2)}) %collective-permute-start.5) | collective-permute-done | bytes 1048608 | tf_op jit(solution)/shard_map/ppermute | solution.py:276
  30.3 2.0 collective-permute-done.refs_3_.refs_2_.refs_4_
  32.3 1.0 copy-done.1
  33.3 5.6 %choose_panel.5 = (bf16[2048,256]{1,0:T(8,128)(2,1)}, bf16[2048,256]{1,0:T(8,128)(2,1)}, bf16[512,2048]{1,0:T(8,128)(2,1)}) custom-call(s32[2]{0:T(128)} %broadcast_select_fusion.1.which_ref, f32[2048,128]{1,0:T(8,128)} %get-tuple-element.146.refs_0_, f32[2048,128]{1,0:T(8,128)} %get-tuple-element.145.refs_1_, ...), custom_call_target="tpu_custom_call" | custom-call | flops 32768 | bytes 98304 | tf_op jit(solution)/shard_map/choose_panel/pallas_call | solution.py:126
  38.9 5.0 %products.14 = (f32[128,512]{1,0:T(8,128)}, f32[128,512]{1,0:T(8,128)}) custom-call(bf16[512,2048]{1,0:T(8,128)(2,1)} %get-tuple-element.75.flipped_ref, bf16[2048,2048]{1,0:T(8,128)(2,1)} %get-tuple-element.76.high_ref, bf16[2048,2048]{1,0:T(8,128)(2,1)} %get-tuple-element.77.low_ref), custom_call_target="tpu_custom_call" | custom-call | flops 25165824 | bytes 98304 | tf_op jit(solution)/shard_map/products/pallas_call | solution.py:155
  43.8 5.3 %products.13 = (f32[128,512]{1,0:T(8,128)}, f32[128,512]{1,0:T(8,128)}) custom-call(bf16[512,2048]{1,0:T(8,128)(2,1)} %get-tuple-element.75.flipped_ref, bf16[2048,2048]{1,0:T(8,128)(2,1)} %get-tuple-element.76.high_ref, bf16[2048,2048]{1,0:T(8,128)(2,1)} %get-tuple-element.77.low_ref), custom_call_target="tpu_custom_call" | custom-call | flops 25165824 | bytes 98304 | tf_op jit(solution)/shard_map/products/pallas_call | solution.py:155
  49.6 1.4 collective-permute-done.6.refs_1_
  51.7 2.3 exchange.9
  54.0 1.6 collective-permute-start.10
  55.6 4.9 %products.16 = (f32[128,512]{1,0:T(8,128)}, f32[128,512]{1,0:T(8,128)}) custom-call(bf16[512,2048]{1,0:T(8,128)(2,1)} %get-tuple-element.75.flipped_ref, bf16[2048,2048]{1,0:T(8,128)(2,1)} %get-tuple-element.76.high_ref, bf16[2048,2048]{1,0:T(8,128)(2,1)} %get-tuple-element.77.low_ref, f32[128,1024]{1,0:T(8,128)} %get-tuple-element.82.refs_0_.refs_5_), custom_call_target="tpu_custom_call" | custom-call | flops 25165824 | bytes 98304 | tf_op jit(solution)/shard_map/products/pallas_call | solution.py:155
  60.6 4.9 %products.15 = (f32[128,512]{1,0:T(8,128)}, f32[128,512]{1,0:T(8,128)}) custom-call(bf16[512,2048]{1,0:T(8,128)(2,1)} %get-tuple-element.75.flipped_ref, bf16[2048,2048]{1,0:T(8,128)(2,1)} %get-tuple-element.76.high_ref, bf16[2048,2048]{1,0:T(8,128)(2,1)} %get-tuple-element.77.low_ref, f32[128,1024]{1,0:T(8,128)} %get-tuple-element.82.refs_0_.refs_5_), custom_call_target="tpu_custom_call" | custom-call | flops 25165824 | bytes 98304 | tf_op jit(solution)/shard_map/products/pallas_call | solution.py:155
  66.1 1.3 collective-permute-done.8.refs_1_
  67.4 1.0 collective-permute-done.10.refs_4_
  69.2 2.7 exchange.10
  71.9 1.6 collective-permute-start.13
  73.5 1.5 collective-permute-start.14
  75.6 0.9 copy-done
  76.9 5.7 %choose_panel.6 = (bf16[2048,256]{1,0:T(8,128)(2,1)}, bf16[2048,256]{1,0:T(8,128)(2,1)}, bf16[512,2048]{1,0:T(8,128)(2,1)}) custom-call(s32[2]{0:T(128)} %broadcast_select_fusion.2.which_ref, f32[2048,128]{1,0:T(8,128)} %collective-permute-done.5.refs_2_.refs_0_, f32[2048,128]{1,0:T(8,128)} %copy-done.3, f32[2048,128]{1,0:T(8,128)} %copy-done.1, ...), custom_call_target="tpu_custom_call" | custom-call | flops 32768 | bytes 98304 | tf_op jit(solution)/shard_map/choose_panel/pallas_call | solution.py:126
  82.6 5.0 %products.18 = (f32[128,512]{1,0:T(8,128)}, f32[128,512]{1,0:T(8,128)}) custom-call(bf16[512,2048]{1,0:T(8,128)(2,1)} %get-tuple-element.89.flipped_ref, bf16[2048,2048]{1,0:T(8,128)(2,1)} %get-tuple-element.76.high_ref, bf16[2048,2048]{1,0:T(8,128)(2,1)} %get-tuple-element.77.low_ref, f32[128,1024]{1,0:T(8,128)} %get-tuple-element.88.refs_4_.refs_0_.refs_6_.refs_5_), custom_call_target="tpu_custom_call" | custom-call | flops 25165824 | bytes 98304 | tf_op jit(solution)/shard_map/products/pallas_call | solution.py:155
  90.3 5.4 %products.17 = (f32[128,512]{1,0:T(8,128)}, f32[128,512]{1,0:T(8,128)}) custom-call(bf16[512,2048]{1,0:T(8,128)(2,1)} %get-tuple-element.89.flipped_ref, bf16[2048,2048]{1,0:T(8,128)(2,1)} %get-tuple-element.76.high_ref, bf16[2048,2048]{1,0:T(8,128)(2,1)} %get-tuple-element.77.low_ref, f32[128,1024]{1,0:T(8,128)} %get-tuple-element.88.refs_4_.refs_0_.refs_6_.refs_5_), custom_call_target="tpu_custom_call" | custom-call | flops 25165824 | bytes 98304 | tf_op jit(solution)/shard_map/products/pallas_call | solution.py:155
  96.7 1.5 collective-permute-start.3
  99.5 5.2 %choose_panel.7.flipped_ref = bf16[512,2048]{1,0:T(8,128)(2,1)} custom-call(s32[2]{0:T(128)} %broadcast_select_fusion.which_ref, f32[2048,128]{1,0:T(8,128)} %get-tuple-element.146.refs_0_, f32[2048,128]{1,0:T(8,128)} %get-tuple-element.145.refs_1_, f32[2048,128]{1,0:T(8,128)} %collective-permute-done.5.refs_2_.refs_0_, f32[2048,128]{1,0:T(8,128)} %copy-done.3, ...), custom_call_target="tpu_custom_call" | custom-call | flops 32768 | bytes 98304 | tf_op jit(solution)/shard_map/choose_panel/pallas_call | solution.py:126
  104.6 4.7 %choose_panel.8 = (bf16[2048,256]{1,0:T(8,128)(2,1)}, bf16[2048,256]{1,0:T(8,128)(2,1)}) custom-call(s32[2]{0:T(128)} %iota_add_fusion.which_ref, f32[2048,128]{1,0:T(8,128)} %get-tuple-element.146.refs_0_, f32[2048,128]{1,0:T(8,128)} %get-tuple-element.145.refs_1_, f32[2048,128]{1,0:T(8,128)} %collective-permute-done.5.refs_2_.refs_0_, ...), custom_call_target="tpu_custom_call" | custom-call | flops 32768 | bytes 98304 | tf_op jit(solution)/shard_map/choose_panel/pallas_call | solution.py:126
  109.3 3.8 %products.19 = (f32[128,256]{1,0:T(8,128)}, f32[128,256]{1,0:T(8,128)}) custom-call(bf16[512,2048]{1,0:T(8,128)(2,1)} %choose_panel.7.flipped_ref, bf16[2048,256]{1,0:T(8,128)(2,1)} %get-tuple-element.96.high_ref, bf16[2048,256]{1,0:T(8,128)(2,1)} %get-tuple-element.97.low_ref), custom_call_target="tpu_custom_call" | custom-call | flops 12582912 | bytes 65536 | tf_op jit(solution)/shard_map/products/pallas_call | solution.py:155
  113.9 3.2 %exchange.11 = (f32[128,1024]{1,0:T(8,128)}, f32[128,1024]{1,0:T(8,128)}, f32[128,1024]{1,0:T(8,128)}, f32[128,1024]{1,0:T(8,128)}) custom-call(s32[1]{0:T(128)} %bitcast.3.ends_ref, f32[128,512]{1,0:T(8,128)} %get-tuple-element.90.refs_0_, f32[128,512]{1,0:T(8,128)} %copy-done.37, f32[128,512]{1,0:T(8,128)} %get-tuple-element.92.refs_2_, ...), custom_call_target="tpu_custom_call" | custom-call | tf_op jit(solution)/shard_map/exchange/pallas_call | solution.py:351
  117.1 5.0 %products.21 = (f32[128,512]{1,0:T(8,128)}, f32[128,512]{1,0:T(8,128)}) custom-call(bf16[512,2048]{1,0:T(8,128)(2,1)} %get-tuple-element.89.flipped_ref, bf16[2048,2048]{1,0:T(8,128)(2,1)} %get-tuple-element.76.high_ref, bf16[2048,2048]{1,0:T(8,128)(2,1)} %get-tuple-element.77.low_ref, f32[128,1024]{1,0:T(8,128)} %get-tuple-element.99.refs_0_.refs_7_), custom_call_target="tpu_custom_call" | custom-call | flops 25165824 | bytes 98304 | tf_op jit(solution)/shard_map/products/pallas_call | solution.py:155
  122.1 3.7 %collective-permute-start.18 = (f32[128,1024]{1,0:T(8,128)S(1)}, f32[128,1024]{1,0:T(8,128)S(1)}, u32[]{:S(2)}, u32[]{:S(2)}) collective-permute-start(f32[128,1024]{1,0:T(8,128)S(1)} %copy-done.45), channel_id=1, source_target_pairs={{0,8},{4,12},{8,0},{12,4},{16,24},{20,28},{24,16},{28,20},{1,9},{5... | collective-permute-start | bytes 1572872 | tf_op jit(solution)/shard_map/ppermute | solution.py:427
  126.7 5.0 %products.20 = (f32[128,512]{1,0:T(8,128)}, f32[128,512]{1,0:T(8,128)}) custom-call(bf16[512,2048]{1,0:T(8,128)(2,1)} %get-tuple-element.89.flipped_ref, bf16[2048,2048]{1,0:T(8,128)(2,1)} %get-tuple-element.76.high_ref, bf16[2048,2048]{1,0:T(8,128)(2,1)} %get-tuple-element.77.low_ref, f32[128,1024]{1,0:T(8,128)} %get-tuple-element.99.refs_0_.refs_7_), custom_call_target="tpu_custom_call" | custom-call | flops 25165824 | bytes 98304 | tf_op jit(solution)/shard_map/products/pallas_call | solution.py:155
  131.9 1.6 collective-permute-done.15.refs_1_
  133.5 4.8 %collective-permute-done.18.refs_6_ = f32[128,1024]{1,0:T(8,128)S(1)} collective-permute-done((f32[128,1024]{1,0:T(8,128)S(1)}, f32[128,1024]{1,0:T(8,128)S(1)}, u32[]{:S(2)}, u32[]{:S(2)}) %collective-permute-start.18) | collective-permute-done | bytes 524320 | tf_op jit(solution)/shard_map/ppermute | solution.py:427
  139.3 3.7 %exchange.12 = (f32[128,1280]{1,0:T(8,128)}, f32[128,1024]{1,0:T(8,128)}, f32[128,1024]{1,0:T(8,128)}, f32[128,1024]{1,0:T(8,128)}, f32[128,1280]{1,0:T(8,128)}) custom-call(s32[1]{0:T(128)} %bitcast.3.ends_ref, f32[128,512]{1,0:T(8,128)} %get-tuple-element.100.refs_0_, f32[128,512]{1,0:T(8,128)} %copy-done.32, f32[128,512]{1,0:T(8,128)} %get-tuple-element.102.refs_2_, ...), custom_call_target="tpu_custom_call" | custom-call | tf_op jit(solution)/shard_map/exchange/pallas_call | solution.py:351
  143.0 3.5 %collective-permute-start.22 = (f32[128,1280]{1,0:T(8,128)}, f32[128,1280]{1,0:T(8,128)}, u32[]{:S(2)}, u32[]{:S(2)}) collective-permute-start(f32[128,1280]{1,0:T(8,128)} %get-tuple-element.114), channel_id=1, source_target_pairs={{0,8},{4,12},{8,0},{12,4},{16,24},{20,28},{24,16},{28,20},{1,9},{5... | collective-permute-start | bytes 1966088 | tf_op jit(solution)/shard_map/ppermute | solution.py:427
  146.5 1.5 collective-permute-start.23
  148.7 1.0 copy-done.5
  149.6 5.7 %choose_panel.9 = (bf16[2048,256]{1,0:T(8,128)(2,1)}, bf16[2048,256]{1,0:T(8,128)(2,1)}, bf16[512,2048]{1,0:T(8,128)(2,1)}) custom-call(s32[2]{0:T(128)} %broadcast_select_fusion.3.which_ref, f32[2048,128]{1,0:T(8,128)} %collective-permute-done.1.refs_0_, f32[2048,128]{1,0:T(8,128)} %copy-done.5, f32[2048,128]{1,0:T(8,128)} %copy-done.3, ...), custom_call_target="tpu_custom_call" | custom-call | flops 32768 | bytes 98304 | tf_op jit(solution)/shard_map/choose_panel/pallas_call | solution.py:126
  155.4 5.0 %products.23 = (f32[128,512]{1,0:T(8,128)}, f32[128,512]{1,0:T(8,128)}) custom-call(bf16[512,2048]{1,0:T(8,128)(2,1)} %get-tuple-element.109.flipped_ref, bf16[2048,2048]{1,0:T(8,128)(2,1)} %get-tuple-element.76.high_ref, bf16[2048,2048]{1,0:T(8,128)(2,1)} %get-tuple-element.77.low_ref, f32[128,1280]{1,0:T(8,128)} %get-tuple-element.108.refs_4_.refs_0_.refs_5_), custom_call_target="tpu_custom_call" | custom-call | flops 25165824 | bytes 98304 | tf_op jit(solution)/shard_map/products/pallas_call | solution.py:155
  160.3 5.3 %products.22 = (f32[128,512]{1,0:T(8,128)}, f32[128,512]{1,0:T(8,128)}) custom-call(bf16[512,2048]{1,0:T(8,128)(2,1)} %get-tuple-element.109.flipped_ref, bf16[2048,2048]{1,0:T(8,128)(2,1)} %get-tuple-element.76.high_ref, bf16[2048,2048]{1,0:T(8,128)(2,1)} %get-tuple-element.77.low_ref, f32[128,1280]{1,0:T(8,128)} %get-tuple-element.108.refs_4_.refs_0_.refs_5_), custom_call_target="tpu_custom_call" | custom-call | flops 25165824 | bytes 98304 | tf_op jit(solution)/shard_map/products/pallas_call | solution.py:155
  166.1 1.4 collective-permute-done.20.refs_1_
  168.2 3.8 %exchange.13 = (f32[128,1024]{1,0:T(8,128)}, f32[128,1280]{1,0:T(8,128)}, f32[128,1024]{1,0:T(8,128)}, f32[128,1024]{1,0:T(8,128)}, f32[128,1024]{1,0:T(8,128)}) custom-call(s32[1]{0:T(128)} %bitcast.3.ends_ref, f32[128,512]{1,0:T(8,128)} %get-tuple-element.110.refs_0_, f32[128,512]{1,0:T(8,128)} %copy-done.30, f32[128,512]{1,0:T(8,128)} %get-tuple-element.112.refs_2_, ...), custom_call_target="tpu_custom_call" | custom-call | tf_op jit(solution)/shard_map/exchange/pallas_call | solution.py:351
  172.7 3.8 %collective-permute-start.27 = (f32[128,1024]{1,0:T(8,128)}, f32[128,1024]{1,0:T(8,128)S(1)}, u32[]{:S(2)}, u32[]{:S(2)}) collective-permute-start(f32[128,1024]{1,0:T(8,128)} %get-tuple-element.123), channel_id=1, source_target_pairs={{0,8},{4,12},{8,0},{12,4},{16,24},{20,28},{24,16},{28,20},{1,9},{5... | collective-permute-start | bytes 1572872 | tf_op jit(solution)/shard_map/ppermute | solution.py:427
  176.4 4.9 %products.25 = (f32[128,512]{1,0:T(8,128)}, f32[128,512]{1,0:T(8,128)}) custom-call(bf16[512,2048]{1,0:T(8,128)(2,1)} %get-tuple-element.109.flipped_ref, bf16[2048,2048]{1,0:T(8,128)(2,1)} %get-tuple-element.76.high_ref, bf16[2048,2048]{1,0:T(8,128)(2,1)} %get-tuple-element.77.low_ref, f32[128,1024]{1,0:T(8,128)} %get-tuple-element.118.refs_0_.refs_5_), custom_call_target="tpu_custom_call" | custom-call | flops 25165824 | bytes 98304 | tf_op jit(solution)/shard_map/products/pallas_call | solution.py:155
  181.4 5.0 %products.24 = (f32[128,512]{1,0:T(8,128)}, f32[128,512]{1,0:T(8,128)}) custom-call(bf16[512,2048]{1,0:T(8,128)(2,1)} %get-tuple-element.109.flipped_ref, bf16[2048,2048]{1,0:T(8,128)(2,1)} %get-tuple-element.76.high_ref, bf16[2048,2048]{1,0:T(8,128)(2,1)} %get-tuple-element.77.low_ref, f32[128,1024]{1,0:T(8,128)} %get-tuple-element.118.refs_0_.refs_5_), custom_call_target="tpu_custom_call" | custom-call | flops 25165824 | bytes 98304 | tf_op jit(solution)/shard_map/products/pallas_call | solution.py:155
  186.8 1.4 collective-permute-done.25.refs_1_
  189.8 3.7 %exchange.14 = (f32[128,1024]{1,0:T(8,128)}, f32[128,1024]{1,0:T(8,128)}, f32[128,1280]{1,0:T(8,128)}, f32[128,1024]{1,0:T(8,128)}, f32[128,1280]{1,0:T(8,128)}) custom-call(s32[1]{0:T(128)} %bitcast.3.ends_ref, f32[128,512]{1,0:T(8,128)} %get-tuple-element.119.refs_0_, f32[128,512]{1,0:T(8,128)} %copy-done.31, f32[128,512]{1,0:T(8,128)} %get-tuple-element.121.refs_2_, ...), custom_call_target="tpu_custom_call" | custom-call | tf_op jit(solution)/shard_map/exchange/pallas_call | solution.py:351
  193.5 2.9 collective-permute-start.29
  197.1 14.0 %collective-permute-done.29.refs_0_ = f32[128,1280]{1,0:T(8,128)S(1)} collective-permute-done((f32[128,1280]{1,0:T(8,128)}, f32[128,1280]{1,0:T(8,128)S(1)}, u32[]{:S(2)}, u32[]{:S(2)}) %collective-permute-start.29) | collective-permute-done | bytes 655392 | tf_op jit(solution)/shard_map/ppermute | solution.py:427
  211.9 3.1 %exchange.15 = (f32[128,1024]{1,0:T(8,128)}, f32[128,1024]{1,0:T(8,128)}, f32[128,1280]{1,0:T(8,128)}, f32[128,1024]{1,0:T(8,128)}) custom-call(s32[1]{0:T(128)} %bitcast.3.ends_ref, f32[128,1280]{1,0:T(8,128)} %copy-done.8, f32[128,1024]{1,0:T(8,128)} %get-tuple-element.127.refs_1_, f32[128,1024]{1,0:T(8,128)} %get-tuple-element.128.refs_2_, ...), custom_call_target="tpu_custom_call" | custom-call | tf_op jit(solution)/shard_map/exchange/pallas_call | solution.py:351
  217.0 1.8 collective-permute-start.32
  219.8 1.5 collective-permute-start.40
  221.5 1.5 collective-permute-start.39
  223.5 1.3 broadcast_select_fusion.4.place_ref
  224.9 6.7 %collective-permute-done.32.refs_0_ = f32[128,1024]{1,0:T(8,128)S(1)} collective-permute-done((f32[128,1024]{1,0:T(8,128)}, f32[128,1024]{1,0:T(8,128)S(1)}, u32[]{:S(2)}, u32[]{:S(2)}) %collective-permute-start.32) | collective-permute-done | bytes 524320 | tf_op jit(solution)/shard_map/ppermute | solution.py:427
  232.5 2.7 exchange.16
  236.3 3.1 %collective-permute-start.34 = (f32[128,1024]{1,0:T(8,128)}, f32[128,1024]{1,0:T(8,128)S(1)}, u32[]{:S(2)}, u32[]{:S(2)}) collective-permute-start(f32[128,1024]{1,0:T(8,128)} %get-tuple-element.134), channel_id=1, source_target_pairs={{0,8},{4,12},{8,0},{12,4},{16,24},{20,28},{24,16},{28,20},{1,9},{5... | collective-permute-start | bytes 1572872 | tf_op jit(solution)/shard_map/ppermute | solution.py:427
  246.3 1.1 select_bitcast_fusion.2
  247.4 0.9 pad_maximum_fusion.refs_7_
  249.5 20.5 %update.2.refs_2_.refs_15_ = f32[2048,2048]{1,0:T(8,128)} custom-call(s32[6]{0:T(128)} %broadcast_select_fusion.4.place_ref, f32[128,1024]{1,0:T(8,128)} %get-tuple-element.136.refs_0_, f32[128,1024]{1,0:T(8,128)} %copy-done.12, f32[128,1024]{1,0:T(8,128)} %get-tuple-element.137.refs_2_, f32[128,1024]{1,0:T(8,128)} %copy-done.13, ...), custom_call_target="tpu_custom_call" | custom-call | flops 150994944 | bytes 360448 | tf_op jit(solution)/shard_map/update/pallas_call | solution.py:219
  270.7 2.1 exchange.17.refs_4_
  273.1 1.8 collective-permute-done.41.refs_5_
  275.7 20.4 %update.3 = f32[2048,2048]{1,0:T(8,128)} custom-call(s32[6]{0:T(128)} %broadcast_select_fusion.4.place_ref, f32[128,1024]{1,0:T(8,128)} %get-tuple-element.117.refs_0_, f32[128,1024]{1,0:T(8,128)} %copy-done.15, f32[128,1280]{1,0:T(8,128)} %get-tuple-element.130.refs_2_, f32[128,1280]{1,0:T(8,128)} %copy-done.6, ...), custom_call_target="tpu_custom_call", output_to_operand_aliasing={{}: (16, {})} | custom-call | flops 150994944 | bytes 360448 | tf_op jit(solution)/shard_map/update/pallas_call | solution.py:219
  (171 shorter events, 26.9 us)
Async XLA Ops:
  0.0 8.1 %copy-start.39 = (s32[3]{0:T(128)S(1)}, s32[3]{0:T(128)}, u32[]{:S(2)}) copy-start(s32[3]{0:T(128)} %param.14) | copy-start | bytes 40
  0.0 8.2 %copy-start.44 = (s32[4,2]{1,0:T(4,128)S(1)}, s32[4,2]{1,0:T(4,128)}, u32[]{:S(2)}) copy-start(s32[4,2]{1,0:T(4,128)} %constant.99.clone) | copy-start | bytes 100
  3.1 27.2 %collective-permute-start.5 = (f32[2048,128]{1,0:T(8,128)}, f32[2048,128]{1,0:T(8,128)}, u32[]{:S(2)}, u32[]{:S(2)}) collective-permute-start(f32[2048,128]{1,0:T(8,128)} %get-tuple-element.146.refs_0_), channel_id=1, source_target_pairs={{0,1},{1,0},{2,3},{3,2},{4,5},{5,4},{6,7},{7,6},{8,9},{9,8},{10,11... | collective-permute-start | bytes 3145736 | tf_op jit(solution)/shard_map/ppermute | solution.py:276
  6.0 26.3 %collective-permute-start = (f32[2048,128]{1,0:T(8,128)}, f32[2048,128]{1,0:T(8,128)S(1)}, u32[]{:S(2)}, u32[]{:S(2)}) collective-permute-start(f32[2048,128]{1,0:T(8,128)} %get-tuple-element.146.refs_0_), channel_id=1, source_target_pairs={{0,2},{1,3},{2,0},{3,1},{4,6},{5,7},{6,4},{7,5},{8,10},{9,11},{10,... | collective-permute-start | bytes 3145736 | tf_op jit(solution)/shard_map/ppermute | solution.py:276
  7.5 68.0 %collective-permute-start.4 = (f32[2048,128]{1,0:T(8,128)}, f32[2048,128]{1,0:T(8,128)S(1)}, u32[]{:S(2)}, u32[]{:S(2)}) collective-permute-start(f32[2048,128]{1,0:T(8,128)} %get-tuple-element.145.refs_1_), channel_id=1, source_target_pairs={{0,2},{1,3},{2,0},{3,1},{4,6},{5,7},{6,4},{7,5},{8,10},{9,11},{10,... | collective-permute-start | bytes 3145736 | tf_op jit(solution)/shard_map/ppermute | solution.py:276
  8.0 67.5 %collective-permute-start.2 = (f32[2048,128]{1,0:T(8,128)}, f32[2048,128]{1,0:T(8,128)S(1)}, u32[]{:S(2)}, u32[]{:S(2)}) collective-permute-start(f32[2048,128]{1,0:T(8,128)} %get-tuple-element.145.refs_1_), channel_id=1, source_target_pairs={{0,1},{1,0},{2,3},{3,2},{4,5},{5,4},{6,7},{7,6},{8,9},{9,8},{10,11... | collective-permute-start | bytes 3145736 | tf_op jit(solution)/shard_map/ppermute | solution.py:276
  43.8 5.8 %collective-permute-start.7 = (f32[128,512]{1,0:T(8,128)}, f32[128,512]{1,0:T(8,128)S(1)}, u32[]{:S(2)}, u32[]{:S(2)}) collective-permute-start(f32[128,512]{1,0:T(8,128)} %get-tuple-element.81), channel_id=1, source_target_pairs={{0,4},{4,0},{8,12},{12,8},{16,20},{20,16},{24,28},{28,24},{1,5},{5... | collective-permute-start | bytes 786440 | tf_op jit(solution)/shard_map/ppermute | solution.py:246
  49.1 1.9 collective-permute-start.6
  54.0 14.4 %collective-permute-start.10 = (f32[128,1024]{1,0:T(8,128)}, f32[128,1024]{1,0:T(8,128)S(1)}, u32[]{:S(2)}, u32[]{:S(2)}) collective-permute-start(f32[128,1024]{1,0:T(8,128)} %get-tuple-element.87), channel_id=1, source_target_pairs={{0,8},{4,12},{8,0},{12,4},{16,24},{20,28},{24,16},{28,20},{1,9},{5... | collective-permute-start | bytes 1572872 | tf_op jit(solution)/shard_map/ppermute | solution.py:427
  60.5 5.5 %copy-start.40 = (s32[4,2]{1,0:T(4,128)S(1)}, s32[4,2]{1,0:T(4,128)}, u32[]{:S(2)}) copy-start(s32[4,2]{1,0:T(4,128)} %constant.101.clone) | copy-start | bytes 100
  60.5 5.5 %copy-start.41 = (s32[4,2]{1,0:T(4,128)S(1)}, s32[4,2]{1,0:T(4,128)}, u32[]{:S(2)}) copy-start(s32[4,2]{1,0:T(4,128)} %constant.100.clone) | copy-start | bytes 100
  60.5 5.6 %collective-permute-start.9 = (f32[128,512]{1,0:T(8,128)}, f32[128,512]{1,0:T(8,128)S(1)}, u32[]{:S(2)}, u32[]{:S(2)}) collective-permute-start(f32[128,512]{1,0:T(8,128)} %get-tuple-element.86), channel_id=1, source_target_pairs={{0,4},{4,0},{8,12},{12,8},{16,20},{20,16},{24,28},{28,24},{1,5},{5... | collective-permute-start | bytes 786440 | tf_op jit(solution)/shard_map/ppermute | solution.py:246
  65.6 1.8 collective-permute-start.8
  66.1 2.3 copy-start.29
  71.9 41.3 %collective-permute-start.13 = (f32[128,1024]{1,0:T(8,128)}, f32[128,1024]{1,0:T(8,128)}, u32[]{:S(2)}, u32[]{:S(2)}) collective-permute-start(f32[128,1024]{1,0:T(8,128)} %get-tuple-element.94), channel_id=1, source_target_pairs={{0,8},{4,12},{8,0},{12,4},{16,24},{20,28},{24,16},{28,20},{1,9},{5... | collective-permute-start | bytes 1572872 | tf_op jit(solution)/shard_map/ppermute | solution.py:427
  73.5 39.7 %collective-permute-start.14 = (f32[128,1024]{1,0:T(8,128)}, f32[128,1024]{1,0:T(8,128)}, u32[]{:S(2)}, u32[]{:S(2)}) collective-permute-start(f32[128,1024]{1,0:T(8,128)} %get-tuple-element.95.refs_6_), channel_id=1, source_target_pairs={{8,16},{12,20},{16,8},{20,12},{9,17},{13,21},{17,9},{21,13},{10,18... | collective-permute-start | bytes 1572872 | tf_op jit(solution)/shard_map/ppermute | solution.py:432
  82.6 5.1 %copy-start.43 = (s32[2,4]{1,0:T(2,128)S(1)}, s32[2,4]{1,0:T(2,128)}, u32[]{:S(2)}) copy-start(s32[2,4]{1,0:T(2,128)} %constant.105.clone) | copy-start | bytes 100
  82.6 5.7 %copy-start.42 = (s32[2,4]{1,0:T(2,128)S(1)}, s32[2,4]{1,0:T(2,128)}, u32[]{:S(2)}) copy-start(s32[2,4]{1,0:T(2,128)} %constant.104.clone) | copy-start | bytes 100
  87.6 10.7 %collective-permute-start.12 = (f32[128,512]{1,0:T(8,128)}, f32[128,512]{1,0:T(8,128)S(1)}, u32[]{:S(2)}, u32[]{:S(2)}) collective-permute-start(f32[128,512]{1,0:T(8,128)} %get-tuple-element.93), channel_id=1, source_target_pairs={{0,4},{4,0},{8,12},{12,8},{16,20},{20,16},{24,28},{28,24},{1,5},{5... | collective-permute-start | bytes 786440 | tf_op jit(solution)/shard_map/ppermute | solution.py:246
  90.3 6.4 %copy-start.4 = (f32[2048,128]{1,0:T(8,128)S(1)}, f32[2048,128]{1,0:T(8,128)}, u32[]{:S(2)}) copy-start(f32[2048,128]{1,0:T(8,128)} %copy-done.3) | copy-start | bytes 3145732
  90.3 8.0 %copy-start.2 = (f32[2048,128]{1,0:T(8,128)S(1)}, f32[2048,128]{1,0:T(8,128)}, u32[]{:S(2)}) copy-start(f32[2048,128]{1,0:T(8,128)} %copy-done.1) | copy-start | bytes 3145732
  95.7 17.4 %collective-permute-start.11 = (f32[128,512]{1,0:T(8,128)}, f32[128,512]{1,0:T(8,128)S(1)}, u32[]{:S(2)}, u32[]{:S(2)}) collective-permute-start(f32[128,512]{1,0:T(8,128)} %get-tuple-element.91), channel_id=1, source_target_pairs={{0,4},{4,0},{8,12},{12,8},{16,20},{20,16},{24,28},{28,24},{1,5},{5... | collective-permute-start | bytes 786440 | tf_op jit(solution)/shard_map/ppermute | solution.py:246
  96.7 51.9 %collective-permute-start.3 = (f32[2048,128]{1,0:T(8,128)S(1)}, f32[2048,128]{1,0:T(8,128)S(1)}, u32[]{:S(2)}, u32[]{:S(2)}) collective-permute-start(f32[2048,128]{1,0:T(8,128)S(1)} %copy-done.4), channel_id=1, source_target_pairs={{0,2},{1,3},{2,0},{3,1},{4,6},{5,7},{6,4},{7,5},{8,10},{9,11},{10,... | collective-permute-start | bytes 3145736 | tf_op jit(solution)/shard_map/ppermute | solution.py:276
  98.3 6.4 %copy-start.36 = (f32[128,512]{1,0:T(8,128)}, f32[128,512]{1,0:T(8,128)S(1)}, u32[]{:S(2)}) copy-start(f32[128,512]{1,0:T(8,128)S(1)} %collective-permute-done.12.refs_3_) | copy-start | bytes 786436
  98.3 50.4 %collective-permute-start.1 = (f32[2048,128]{1,0:T(8,128)S(1)}, f32[2048,128]{1,0:T(8,128)}, u32[]{:S(2)}, u32[]{:S(2)}) collective-permute-start(f32[2048,128]{1,0:T(8,128)S(1)} %copy-done.2), channel_id=1, source_target_pairs={{0,1},{1,0},{2,3},{3,2},{4,5},{5,4},{6,7},{7,6},{8,9},{9,8},{10,11... | collective-permute-start | bytes 3145736 | tf_op jit(solution)/shard_map/ppermute | solution.py:276
  113.2 12.6 %collective-permute-start.17 = (f32[128,256]{1,0:T(8,128)}, f32[128,256]{1,0:T(8,128)S(1)}, u32[]{:S(2)}, u32[]{:S(2)}) collective-permute-start(f32[128,256]{1,0:T(8,128)} %get-tuple-element.104), channel_id=1, source_target_pairs={{0,4},{4,0},{8,12},{12,8},{16,20},{20,16},{24,28},{28,24},{1,5},{5... | collective-permute-start | bytes 393224 | tf_op jit(solution)/shard_map/ppermute | solution.py:246
  117.1 5.0 %copy-start.45 = (f32[128,1024]{1,0:T(8,128)S(1)}, f32[128,1024]{1,0:T(8,128)}, u32[]{:S(2)}) copy-start(f32[128,1024]{1,0:T(8,128)} %get-tuple-element.105) | copy-start | bytes 1572868
  117.1 8.7 %copy-start.17 = (f32[128,1024]{1,0:T(8,128)S(1)}, f32[128,1024]{1,0:T(8,128)}, u32[]{:S(2)}) copy-start(f32[128,1024]{1,0:T(8,128)} %get-tuple-element.106.refs_8_) | copy-start | bytes 1572868
  122.1 9.6 %collective-permute-start.16 = (f32[128,512]{1,0:T(8,128)}, f32[128,512]{1,0:T(8,128)S(1)}, u32[]{:S(2)}, u32[]{:S(2)}) collective-permute-start(f32[128,512]{1,0:T(8,128)} %get-tuple-element.103), channel_id=1, source_target_pairs={{0,4},{4,0},{8,12},{12,8},{16,20},{20,16},{24,28},{28,24},{1,5},{5... | collective-permute-start | bytes 786440 | tf_op jit(solution)/shard_map/ppermute | solution.py:246
  122.1 16.2 %collective-permute-start.18 = (f32[128,1024]{1,0:T(8,128)S(1)}, f32[128,1024]{1,0:T(8,128)S(1)}, u32[]{:S(2)}, u32[]{:S(2)}) collective-permute-start(f32[128,1024]{1,0:T(8,128)S(1)} %copy-done.45), channel_id=1, source_target_pairs={{0,8},{4,12},{8,0},{12,4},{16,24},{20,28},{24,16},{28,20},{1,9},{5... | collective-permute-start | bytes 1572872 | tf_op jit(solution)/shard_map/ppermute | solution.py:427
  125.8 5.9 %copy-start.38 = (f32[128,256]{1,0:T(8,128)}, f32[128,256]{1,0:T(8,128)S(1)}, u32[]{:S(2)}) copy-start(f32[128,256]{1,0:T(8,128)S(1)} %collective-permute-done.17.refs_5_) | copy-start | bytes 393220
  125.8 12.5 %collective-permute-start.19 = (f32[128,1024]{1,0:T(8,128)S(1)}, f32[128,1024]{1,0:T(8,128)S(1)}, u32[]{:S(2)}, u32[]{:S(2)}) collective-permute-start(f32[128,1024]{1,0:T(8,128)S(1)} %copy-done.17), channel_id=1, source_target_pairs={{8,16},{12,20},{16,8},{20,12},{9,17},{13,21},{17,9},{21,13},{10,18... | collective-permute-start | bytes 1572872 | tf_op jit(solution)/shard_map/ppermute | solution.py:432
  131.7 6.7 %copy-start.26 = (f32[128,512]{1,0:T(8,128)}, f32[128,512]{1,0:T(8,128)S(1)}, u32[]{:S(2)}) copy-start(f32[128,512]{1,0:T(8,128)S(1)} %collective-permute-done.16.refs_3_) | copy-start | bytes 786436
  131.7 1.8 collective-permute-start.15
  133.5 4.8 %copy-start.32 = (f32[128,512]{1,0:T(8,128)}, f32[128,512]{1,0:T(8,128)S(1)}, u32[]{:S(2)}) copy-start(f32[128,512]{1,0:T(8,128)S(1)} %collective-permute-done.15.refs_1_) | copy-start | bytes 786436
  143.0 24.5 %collective-permute-start.22 = (f32[128,1280]{1,0:T(8,128)}, f32[128,1280]{1,0:T(8,128)}, u32[]{:S(2)}, u32[]{:S(2)}) collective-permute-start(f32[128,1280]{1,0:T(8,128)} %get-tuple-element.114), channel_id=1, source_target_pairs={{0,8},{4,12},{8,0},{12,4},{16,24},{20,28},{24,16},{28,20},{1,9},{5... | collective-permute-start | bytes 1966088 | tf_op jit(solution)/shard_map/ppermute | solution.py:427
  146.5 21.0 %collective-permute-start.23 = (f32[128,1024]{1,0:T(8,128)}, f32[128,1024]{1,0:T(8,128)}, u32[]{:S(2)}, u32[]{:S(2)}) collective-permute-start(f32[128,1024]{1,0:T(8,128)} %get-tuple-element.115.refs_6_), channel_id=1, source_target_pairs={{8,16},{12,20},{16,8},{20,12},{9,17},{13,21},{17,9},{21,13},{10,18... | collective-permute-start | bytes 1572872 | tf_op jit(solution)/shard_map/ppermute | solution.py:432
  160.3 5.8 %collective-permute-start.21 = (f32[128,512]{1,0:T(8,128)}, f32[128,512]{1,0:T(8,128)S(1)}, u32[]{:S(2)}, u32[]{:S(2)}) collective-permute-start(f32[128,512]{1,0:T(8,128)} %get-tuple-element.113), channel_id=1, source_target_pairs={{0,4},{4,0},{8,12},{12,8},{16,20},{20,16},{24,28},{28,24},{1,5},{5... | collective-permute-start | bytes 786440 | tf_op jit(solution)/shard_map/ppermute | solution.py:246
  165.6 1.9 collective-permute-start.20
  172.0 16.8 %collective-permute-start.28 = (f32[128,1280]{1,0:T(8,128)}, f32[128,1280]{1,0:T(8,128)S(1)}, u32[]{:S(2)}, u32[]{:S(2)}) collective-permute-start(f32[128,1280]{1,0:T(8,128)} %get-tuple-element.124.refs_6_), channel_id=1, source_target_pairs={{8,16},{12,20},{16,8},{20,12},{9,17},{13,21},{17,9},{21,13},{10,18... | collective-permute-start | bytes 1966088 | tf_op jit(solution)/shard_map/ppermute | solution.py:432
  172.7 16.1 %collective-permute-start.27 = (f32[128,1024]{1,0:T(8,128)}, f32[128,1024]{1,0:T(8,128)S(1)}, u32[]{:S(2)}, u32[]{:S(2)}) collective-permute-start(f32[128,1024]{1,0:T(8,128)} %get-tuple-element.123), channel_id=1, source_target_pairs={{0,8},{4,12},{8,0},{12,4},{16,24},{20,28},{24,16},{28,20},{1,9},{5... | collective-permute-start | bytes 1572872 | tf_op jit(solution)/shard_map/ppermute | solution.py:427
  181.4 5.5 %collective-permute-start.26 = (f32[128,512]{1,0:T(8,128)}, f32[128,512]{1,0:T(8,128)S(1)}, u32[]{:S(2)}, u32[]{:S(2)}) collective-permute-start(f32[128,512]{1,0:T(8,128)} %get-tuple-element.122), channel_id=1, source_target_pairs={{0,4},{4,0},{8,12},{12,8},{16,20},{20,16},{24,28},{28,24},{1,5},{5... | collective-permute-start | bytes 786440 | tf_op jit(solution)/shard_map/ppermute | solution.py:246
  186.4 1.9 collective-permute-start.25
  186.8 2.0 copy-start.27
  193.5 38.0 %copy-start.9 = (f32[128,1024]{1,0:T(8,128)S(1)}, f32[128,1024]{1,0:T(8,128)}, u32[]{:S(2)}) copy-start(f32[128,1024]{1,0:T(8,128)} %get-tuple-element.136.refs_0_) | copy-start | bytes 1572868
  193.5 38.1 %copy-start.11 = (f32[128,1024]{1,0:T(8,128)S(1)}, f32[128,1024]{1,0:T(8,128)}, u32[]{:S(2)}) copy-start(f32[128,1024]{1,0:T(8,128)} %get-tuple-element.137.refs_2_) | copy-start | bytes 1572868
  193.5 17.6 %collective-permute-start.29 = (f32[128,1280]{1,0:T(8,128)}, f32[128,1280]{1,0:T(8,128)S(1)}, u32[]{:S(2)}, u32[]{:S(2)}) collective-permute-start(f32[128,1280]{1,0:T(8,128)} %get-tuple-element.126), channel_id=1, source_target_pairs={{0,8},{4,12},{8,0},{12,4},{16,24},{20,28},{24,16},{28,20},{1,9},{5... | collective-permute-start | bytes 1966088 | tf_op jit(solution)/shard_map/ppermute | solution.py:427
  196.4 0.7 collective-permute-start.30
  197.1 14.0 %copy-start.24 = (f32[128,1024]{1,0:T(8,128)}, f32[128,1024]{1,0:T(8,128)S(1)}, u32[]{:S(2)}) copy-start(f32[128,1024]{1,0:T(8,128)S(1)} %collective-permute-done.30.refs_3_) | copy-start | bytes 1572868
  215.1 30.9 %copy-start.10 = (f32[128,1024]{1,0:T(8,128)S(1)}, f32[128,1024]{1,0:T(8,128)}, u32[]{:S(2)}) copy-start(f32[128,1024]{1,0:T(8,128)} %get-tuple-element.117.refs_0_) | copy-start | bytes 1572868
  215.1 4.6 %collective-permute-start.31 = (f32[128,1280]{1,0:T(8,128)}, f32[128,1280]{1,0:T(8,128)S(1)}, u32[]{:S(2)}, u32[]{:S(2)}) collective-permute-start(f32[128,1280]{1,0:T(8,128)} %get-tuple-element.130.refs_2_), channel_id=1, source_target_pairs={{0,4},{4,0},{8,12},{12,8},{16,20},{20,16},{24,28},{28,24},{1,5},{5... | collective-permute-start | bytes 1966088 | tf_op jit(solution)/shard_map/ppermute | solution.py:246
  217.0 14.6 %collective-permute-start.32 = (f32[128,1024]{1,0:T(8,128)}, f32[128,1024]{1,0:T(8,128)S(1)}, u32[]{:S(2)}, u32[]{:S(2)}) collective-permute-start(f32[128,1024]{1,0:T(8,128)} %get-tuple-element.131), channel_id=1, source_target_pairs={{0,8},{4,12},{8,0},{12,4},{16,24},{20,28},{24,16},{28,20},{1,9},{5... | collective-permute-start | bytes 1572872 | tf_op jit(solution)/shard_map/ppermute | solution.py:427
  218.8 12.8 %collective-permute-start.33 = (f32[128,1024]{1,0:T(8,128)}, f32[128,1024]{1,0:T(8,128)S(1)}, u32[]{:S(2)}, u32[]{:S(2)}) collective-permute-start(f32[128,1024]{1,0:T(8,128)} %get-tuple-element.132.refs_1_), channel_id=1, source_target_pairs={{8,16},{12,20},{16,8},{20,12},{9,17},{13,21},{17,9},{21,13},{10,18... | collective-permute-start | bytes 1572872 | tf_op jit(solution)/shard_map/ppermute | solution.py:432
  219.7 27.6 %copy-start.6 = (f32[128,1280]{1,0:T(8,128)}, f32[128,1280]{1,0:T(8,128)S(1)}, u32[]{:S(2)}) copy-start(f32[128,1280]{1,0:T(8,128)S(1)} %collective-permute-done.31.refs_3_) | copy-start | bytes 1966084
  219.8 15.5 %collective-permute-start.40 = (f32[256,256]{1,0:T(8,128)S(1)}, f32[256,256]{1,0:T(8,128)}, u32[]{:S(2)}, u32[]{:S(2)}) collective-permute-start(f32[256,256]{1,0:T(8,128)S(1)} %maximum_select_fusion), channel_id=1, source_target_pairs={{0,3},{1,2},{2,1},{3,0},{4,7},{5,6},{6,5},{7,4},{8,11},{9,10},{10,... | collective-permute-start | bytes 786440 | tf_op jit(solution)/shard_map/ppermute | solution.py:443
  221.5 14.8 %collective-permute-start.39 = (f32[256,256]{1,0:T(8,128)S(1)}, f32[256,256]{1,0:T(8,128)S(1)}, u32[]{:S(2)}, u32[]{:S(2)}) collective-permute-start(f32[256,256]{1,0:T(8,128)S(1)} %maximum_select_fusion), channel_id=1, source_target_pairs={{0,2},{1,3},{2,0},{3,1},{4,6},{5,7},{6,4},{7,5},{8,10},{9,11},{10,... | collective-permute-start | bytes 786440 | tf_op jit(solution)/shard_map/ppermute | solution.py:443
  223.0 23.0 %collective-permute-start.38 = (f32[256,256]{1,0:T(8,128)S(1)}, f32[256,256]{1,0:T(8,128)S(1)}, u32[]{:S(2)}, u32[]{:S(2)}) collective-permute-start(f32[256,256]{1,0:T(8,128)S(1)} %maximum_select_fusion), channel_id=1, source_target_pairs={{0,1},{1,0},{2,3},{3,2},{4,5},{5,4},{6,7},{7,6},{8,9},{9,8},{10,11... | collective-permute-start | bytes 786440 | tf_op jit(solution)/shard_map/ppermute | solution.py:443
  231.5 16.8 %collective-permute-start.35 = (f32[128,1024]{1,0:T(8,128)S(1)}, f32[128,1024]{1,0:T(8,128)S(1)}, u32[]{:S(2)}, u32[]{:S(2)}) collective-permute-start(f32[128,1024]{1,0:T(8,128)S(1)} %copy-done.9), channel_id=1, source_target_pairs={{0,4},{4,0},{8,12},{12,8},{16,20},{20,16},{24,28},{28,24},{1,5},{5... | collective-permute-start | bytes 1572872 | tf_op jit(solution)/shard_map/ppermute | solution.py:246
  231.6 16.7 %collective-permute-start.36 = (f32[128,1024]{1,0:T(8,128)S(1)}, f32[128,1024]{1,0:T(8,128)S(1)}, u32[]{:S(2)}, u32[]{:S(2)}) collective-permute-start(f32[128,1024]{1,0:T(8,128)S(1)} %copy-done.11), channel_id=1, source_target_pairs={{0,4},{4,0},{8,12},{12,8},{16,20},{20,16},{24,28},{28,24},{1,5},{5... | collective-permute-start | bytes 1572872 | tf_op jit(solution)/shard_map/ppermute | solution.py:246
  235.3 13.1 %collective-permute-start.37 = (f32[128,1024]{1,0:T(8,128)}, f32[128,1024]{1,0:T(8,128)S(1)}, u32[]{:S(2)}, u32[]{:S(2)}) collective-permute-start(f32[128,1024]{1,0:T(8,128)} %get-tuple-element.138.refs_4_), channel_id=1, source_target_pairs={{0,4},{4,0},{8,12},{12,8},{16,20},{20,16},{24,28},{28,24},{1,5},{5... | collective-permute-start | bytes 1572872 | tf_op jit(solution)/shard_map/ppermute | solution.py:246
  236.3 33.6 %collective-permute-start.34 = (f32[128,1024]{1,0:T(8,128)}, f32[128,1024]{1,0:T(8,128)S(1)}, u32[]{:S(2)}, u32[]{:S(2)}) collective-permute-start(f32[128,1024]{1,0:T(8,128)} %get-tuple-element.134), channel_id=1, source_target_pairs={{0,8},{4,12},{8,0},{12,4},{16,24},{20,28},{24,16},{28,20},{1,9},{5... | collective-permute-start | bytes 1572872 | tf_op jit(solution)/shard_map/ppermute | solution.py:427
  246.0 27.1 %collective-permute-start.24 = (f32[128,1024]{1,0:T(8,128)S(1)}, f32[128,1024]{1,0:T(8,128)S(1)}, u32[]{:S(2)}, u32[]{:S(2)}) collective-permute-start(f32[128,1024]{1,0:T(8,128)S(1)} %copy-done.10), channel_id=1, source_target_pairs={{0,4},{4,0},{8,12},{12,8},{16,20},{20,16},{24,28},{28,24},{1,5},{5... | collective-permute-start | bytes 1572872 | tf_op jit(solution)/shard_map/ppermute | solution.py:246
  272.8 2.1 collective-permute-start.41
  273.1 1.8 copy-start.15
  (24 other events, 22.3 us)

commit v2 on v1

--- a/solution.py
+++ b/solution.py
@@ -11,7 +11,7 @@
 BLOCK = 512
 LAG = 1
 PIECE = 512
-VMEM = 54 * 1024 * 1024
+MIB = 1024 * 1024
 F32 = jnp.float32
 BF16 = jnp.bfloat16
 ANYWHERE = pl.BlockSpec(memory_space=pl.ANY)
@@ -29,11 +29,14 @@
 def dot_three(left, right):
     left_high, left_low = split(left)
     right_high, right_low = split(right)
-    return dot(left_high, right_high) + (dot(left_high, right_low) + dot(left_low, right_high))
-
-
-def params():
-    return pltpu.CompilerParams(vmem_limit_bytes=VMEM)
+    return dot(
+        jnp.concatenate([left_high, left_low, left_high], axis=1),
+        jnp.concatenate([right_high, right_high, right_low], axis=0),
+    )
+
+
+def params(mib):
+    return pltpu.CompilerParams(vmem_limit_bytes=mib * MIB)
 
 
 def cost(flops, count):
@@ -54,7 +57,7 @@
         in_specs=[spec],
         out_specs=[spec, spec],
         out_shape=[jax.ShapeDtypeStruct(x.shape, BF16)] * 2,
-        compiler_params=params(),
+        compiler_params=params(16),
         cost_estimate=cost(rows * columns * 4, rows * columns * 8),
         name="split_x",
     )(x)
@@ -85,7 +88,7 @@
             jax.ShapeDtypeStruct((rows, 2 * half), BF16),
             jax.ShapeDtypeStruct((4 * half, rows), BF16),
         ],
-        compiler_params=params(),
+        compiler_params=params(16),
         cost_estimate=cost(rows * half * 8, rows * half * 24),
         name="prepare_panel",
     )(keep, send, *after)
@@ -129,17 +132,17 @@
         out_specs=[in_vmem] * len(outputs),
         out_shape=[jax.ShapeDtypeStruct(shapes[name], BF16) for name in outputs],
         scratch_shapes=[pltpu.VMEM((rows, 2 * half), F32), pltpu.SemaphoreType.DMA],
-        compiler_params=params(),
+        compiler_params=params(14),
         cost_estimate=cost(rows * half * 8, rows * half * 24),
         name="choose_panel",
     )(which, *cases, *after)
 
 
-def products_kernel(flipped_ref, high_ref, low_ref, *refs):
+def products_kernel(columns, flipped_ref, high_ref, low_ref, *refs):
     keep_ref, send_ref = refs[-2:]
     width = flipped_ref.shape[0] // 2
-    with_high = dot(flipped_ref[...], high_ref[...])
-    with_low = dot(flipped_ref[:width, :], low_ref[...])
+    with_high = dot(flipped_ref[...], high_ref[:, columns])
+    with_low = dot(flipped_ref[:width, :], low_ref[:, columns])
     total = with_high[:width] + (with_high[width:] + with_low)
     keep_ref[...] = total[: width // 2]
     send_ref[...] = total[width // 2 :]
@@ -148,18 +151,13 @@
 def products(flipped, high, low, block, width, after=()):
     rows = high.shape[0]
     half = flipped.shape[0] // 4
-    step = min(width, 256)
-    steps = width // step
-    x_spec = pl.BlockSpec((rows, step), lambda i: (0, block * steps + i))
-    out_spec = pl.BlockSpec((half, step), lambda i: (0, i))
+    in_vmem = pl.BlockSpec(memory_space=pltpu.VMEM)
     return pl.pallas_call(
-        products_kernel,
-        grid=(steps,),
-        in_specs=[pl.BlockSpec((4 * half, rows), lambda i: (0, 0)), x_spec, x_spec]
-        + [ANYWHERE] * len(after),
-        out_specs=[out_spec, out_spec],
+        functools.partial(products_kernel, slice(block * width, (block + 1) * width)),
+        in_specs=[in_vmem] * 3 + [ANYWHERE] * len(after),
+        out_specs=[in_vmem] * 2,
         out_shape=[jax.ShapeDtypeStruct((half, width), F32)] * 2,
-        compiler_params=params(),
+        compiler_params=params(28),
         cost_estimate=cost(2 * 6 * half * rows * width, rows * width * 4 + 8 * half * rows),
         name="products",
     )(flipped, high, low, *after)
@@ -170,7 +168,7 @@
     tfac_ref, gram_ref = refs[6:8]
     high_refs, low_refs = refs[8:11], refs[11:14]
     x_ref = refs[14]
-    out_ref, w_ref, y_ref, y_high_ref, y_low_ref = refs[-5:]
+    out_ref, w_ref, y_ref, y_split_ref = refs[-4:]
     half = sums[0].shape[0]
     width = 2 * half
 
@@ -188,13 +186,11 @@
         for index in range(6):
             start = pl.multiple_of(place_ref[index] * half, half)
             high, low = split(y_ref[pl.ds(start, half), :])
-            y_high_ref[index * half : (index + 1) * half, :] = high
-            y_low_ref[index * half : (index + 1) * half, :] = low
-
-    high = jnp.concatenate([ref[...] for ref in high_refs], axis=1)
-    low = jnp.concatenate([ref[...] for ref in low_refs], axis=1)
-    change = dot(high, y_high_ref[...]) + (dot(high, y_low_ref[...]) + dot(low, y_high_ref[...]))
-    out_ref[...] = x_ref[...] - change
+            for number, value in enumerate((high, high, low)):
+                y_split_ref[(6 * number + index) * half : (6 * number + index + 1) * half, :] = value
+
+    sides = [ref[...] for ref in (*high_refs, *low_refs, *high_refs)]
+    out_ref[...] = x_ref[...] - dot(jnp.concatenate(sides, axis=1), y_split_ref[...])
 
 
 def update(place, sums, tfac, grams, highs, lows, x, out, block, width):
@@ -226,13 +222,12 @@
             scratch_shapes=[
                 pltpu.VMEM((6 * half, width), F32),
                 pltpu.VMEM((6 * half, width), F32),
-                pltpu.VMEM((6 * half, width), BF16),
-                pltpu.VMEM((6 * half, width), BF16),
+                pltpu.VMEM((18 * half, width), BF16),
             ],
         ),
         out_shape=jax.ShapeDtypeStruct(x.shape, F32),
         input_output_aliases=aliases,
-        compiler_params=params(),
+        compiler_params=params(40),
         cost_estimate=cost(2 * 18 * half * rows * width, rows * width * 8 + rows * half * 24),
         name="update",
     )(*operands)
@@ -354,7 +349,7 @@
         + [ANYWHERE] * len(after),
         out_specs=[in_vmem] * len(shapes),
         out_shape=[jax.ShapeDtypeStruct(shape, F32) for shape in shapes.values()],
-        compiler_params=params(),
+        compiler_params=params(14),
         cost_estimate=cost(0, 0),
         name="exchange",
     )(ends, *operands.values(), *after)

time: 297 us -> 266 us (0.90)
  Pallas kernels: 174 us -> 89.3 us
  local copies, waits for them, and re-layouts: 18.7 us -> 63.6 us
  waiting for transfers between devices: 45.4 us -> 59.5 us
  other arithmetic: 7.66 us -> 2.11 us
    unnamed x92 -> x114, local copies, waits for them, and re-layouts: 12.1 us -> 58.3 us
    pallas_call x13, Pallas kernels: 64.5 us -> 25.2 us  [products(): pl.pallas_call(functools.partial(products_kernel, slice(block * width, (b...]
    pallas_call x9, Pallas kernels: 27.4 us -> 9.37 us  [exchange(): pl.pallas_call(functools.partial(exchange_kernel, names, pieces), in_spec...]
    pallas_call x1, Pallas kernels: 14 us -> 2.45 us  [split_array(): pl.pallas_call(split_kernel, grid=(rows // step,), in_specs=[spec], out_s...]
    pallas_call x5, Pallas kernels: 26.9 us -> 16.5 us  [choose(): pl.pallas_call(functools.partial(choose_kernel, outputs, len(cases)), in_...]
    ppermute x8, waiting for transfers between devices: 27.1 us -> 35.6 us  [shards_square(): outer[step] = lax.ppermute(results['out'], 'row', outer_pairs)]
    ppermute x6, waiting for transfers between devices: 9.54 us -> 15.6 us  [fetch_square(): along = lambda value, step: lax.ppermute(value, 'col', pairs_of(4, step))]
    pallas_call x2, Pallas kernels: 40.9 us -> 35.8 us  [update(): pl.pallas_call(update_kernel, grid_spec=pltpu.PrefetchScalarGridSpec(num_...]
  transfers between devices with their start and end apart: 42 -> 42, of which waited for: 13 -> 13; matrix products, arithmetic and copies ran while one was open for 4% -> 2% of each run, Pallas kernels for 48% -> 26%
where the time goes in v2:
time: 266 us; the launch traced here: 265 us
  Pallas kernels  89.3 us (34%)
  local copies, waits for them, and re-layouts  63.6 us (24%)
  waiting for transfers between devices  59.5 us (22%)
  starting transfers between devices  42.6 us (16%)
  between operations  7.54 us (3%)
    unnamed x114, local copies, waits for them, and re-layouts  58.3 us
    pallas_call x2, Pallas kernels, update(): pl.pallas_call(update_kernel, grid_spec=pltpu.PrefetchScalarGridSpec(num_...  35.8 us
    ppermute x8, waiting for transfers between devices, shards_square(): outer[step] = lax.ppermute(results['out'], 'row', outer_pairs)  35.6 us
    pallas_call x13, Pallas kernels, products(): pl.pallas_call(functools.partial(products_kernel, slice(block * width, (b...  25.2 us
    ppermute x8, starting transfers between devices, shards_square(): outer[step] = lax.ppermute(results['out'], 'row', outer_pairs)  21.9 us
    pallas_call x5, Pallas kernels, choose(): pl.pallas_call(functools.partial(choose_kernel, outputs, len(cases)), in_...  16.5 us
    ppermute x6, waiting for transfers between devices, fetch_square(): along = lambda value, step: lax.ppermute(value, 'col', pairs_of(4, step))  15.6 us
    pallas_call x9, Pallas kernels, exchange(): pl.pallas_call(functools.partial(exchange_kernel, names, pieces), in_spec...  9.37 us
  transfers between devices with their start and end apart: 42, of which 13 were waited for; matrix products, arithmetic and copies ran while one was open for 2% of the time, Pallas kernels for 26%

profile of v2, /device:TPU:0, one launch (start us, length us, event | category | flops | bytes accessed | tf_op | source)
XLA Modules:
  0.0 264.7 jit_solution(18247389259685371031)
XLA Ops:
  0.0 2.7 %fusion.14 = (f32[2048,128]{1,0:T(8,128)}, f32[2048,128]{1,0:T(8,128)S(1)}) fusion(f32[2048,256]{1,0:T(8,128)} %bitcast.39), kind=kLoop, calls=%fused_computation.37 | loop fusion | bytes 4194304 | tf_op jit(solution)/shard_map/slice | solution.py:272
  2.7 2.9 %collective-permute-start.5 = (f32[2048,128]{1,0:T(8,128)S(1)}, f32[2048,128]{1,0:T(8,128)S(1)}, u32[]{:S(2)}, u32[]{:S(2)}) collective-permute-start(f32[2048,128]{1,0:T(8,128)S(1)} %get-tuple-element.146.refs_0_), channel_id=1, source_target_pairs={{0,1},{1,0},{2,3},{3,2},{4,5},{5,4},{6,7},{7,6},{8,9},{9,8},{10,11... | collective-permute-start | bytes 3145736 | tf_op jit(solution)/shard_map/ppermute | solution.py:271
  5.7 1.5 collective-permute-start
  8.0 5.8 %copy-done.10 = f32[2048,2048]{1,0:T(8,128)S(1)} copy-done((f32[2048,2048]{1,0:T(8,128)S(1)}, f32[2048,2048]{1,0:T(8,128)}, u32[]{:S(2)}) %copy-start.10) | copy-done | bytes 16777240
  13.8 2.5 split_x.1
  16.2 13.4 %collective-permute-done.5.refs_2_.refs_0_ = f32[2048,128]{1,0:T(8,128)S(1)} collective-permute-done((f32[2048,128]{1,0:T(8,128)S(1)}, f32[2048,128]{1,0:T(8,128)S(1)}, u32[]{:S(2)}, u32[]{:S(2)}) %collective-permute-start.5) | collective-permute-done | bytes 1048608 | tf_op jit(solution)/shard_map/ppermute | solution.py:271
  29.7 2.2 collective-permute-done.refs_3_.refs_2_.refs_4_
  31.9 1.2 copy-done.16
  33.1 2.6 choose_panel.5
  37.7 1.8 products.14
  39.5 2.5 products.13
  42.5 1.4 collective-permute-done.6.refs_1_
  46.5 1.6 collective-permute-start.10
  48.1 3.4 %copy-done.1 = bf16[2048,2048]{1,0:T(8,128)(2,1)S(1)} copy-done((bf16[2048,2048]{1,0:T(8,128)(2,1)S(1)}, bf16[2048,2048]{1,0:T(8,128)(2,1)}, u32[]{:S(2)}) %copy-start.1) | copy-done | bytes 8388632
  51.4 3.4 %copy-done.6 = bf16[2048,2048]{1,0:T(8,128)(2,1)S(1)} copy-done((bf16[2048,2048]{1,0:T(8,128)(2,1)S(1)}, bf16[2048,2048]{1,0:T(8,128)(2,1)}, u32[]{:S(2)}) %copy-start.6) | copy-done | bytes 8388632
  54.8 2.5 products.16
  57.4 2.5 products.15
  61.1 1.3 collective-permute-done.8.refs_1_
  65.2 2.1 exchange.10
  67.8 1.5 collective-permute-start.14
  69.3 1.2 copy-done.13
  70.5 3.7 %choose_panel.6 = (bf16[2048,256]{1,0:T(8,128)(2,1)S(1)}, bf16[2048,256]{1,0:T(8,128)(2,1)S(1)}, bf16[512,2048]{1,0:T(8,128)(2,1)S(1)}) custom-call(s32[2]{0:T(128)S(1)} %broadcast_select_fusion.2.which_ref, f32[2048,128]{1,0:T(8,128)S(1)} %copy-done.13, f32[2048,128]{1,0:T(8,128)} %collective-permute-done.2.refs_1_.refs_3_.refs_2_, ...), custom_call_target="tpu_custom_call" | custom-call | flops 32768 | bytes 98304 | tf_op jit(solution)/shard_map/choose_panel/pallas_call | solution.py:129
  76.2 3.4 %copy-done.2 = bf16[2048,2048]{1,0:T(8,128)(2,1)S(1)} copy-done((bf16[2048,2048]{1,0:T(8,128)(2,1)S(1)}, bf16[2048,2048]{1,0:T(8,128)(2,1)}, u32[]{:S(2)}) %copy-start.2) | copy-done | bytes 8388632
  79.6 3.4 %copy-done.7 = bf16[2048,2048]{1,0:T(8,128)(2,1)S(1)} copy-done((bf16[2048,2048]{1,0:T(8,128)(2,1)S(1)}, bf16[2048,2048]{1,0:T(8,128)(2,1)}, u32[]{:S(2)}) %copy-start.7) | copy-done | bytes 8388632
  83.0 2.5 products.18
  88.2 3.4 %copy-done.3 = bf16[2048,2048]{1,0:T(8,128)(2,1)S(1)} copy-done((bf16[2048,2048]{1,0:T(8,128)(2,1)S(1)}, bf16[2048,2048]{1,0:T(8,128)(2,1)}, u32[]{:S(2)}) %copy-start.3) | copy-done | bytes 8388632
  91.6 3.4 %copy-done.8 = bf16[2048,2048]{1,0:T(8,128)(2,1)S(1)} copy-done((bf16[2048,2048]{1,0:T(8,128)(2,1)S(1)}, bf16[2048,2048]{1,0:T(8,128)(2,1)}, u32[]{:S(2)}) %copy-start.8) | copy-done | bytes 8388632
  95.0 1.8 products.17
  98.2 2.9 %choose_panel.7.flipped_ref = bf16[512,2048]{1,0:T(8,128)(2,1)S(1)} custom-call(s32[2]{0:T(128)S(1)} %broadcast_select_fusion.which_ref, f32[2048,128]{1,0:T(8,128)S(1)} %copy-done.17, f32[2048,128]{1,0:T(8,128)} %get-tuple-element.145.refs_1_, f32[2048,128]{1,0:T(8,128)S(1)} %copy-done.14, f32[2048,128]{1,0:T(8,128)} %collective-permute-done.2.refs_1_.refs_3_.refs_2_, ...), custom_call_target="tpu_custom_call" | custom-call | flops 32768 | bytes 98304 | tf_op jit(solution)/shard_map/choose_panel/pallas_call | solution.py:129
  101.1 3.6 %choose_panel.8 = (bf16[2048,256]{1,0:T(8,128)(2,1)S(1)}, bf16[2048,256]{1,0:T(8,128)(2,1)S(1)}) custom-call(s32[2]{0:T(128)S(1)} %iota_add_fusion.which_ref, f32[2048,128]{1,0:T(8,128)S(1)} %copy-done.17, f32[2048,128]{1,0:T(8,128)} %get-tuple-element.145.refs_1_, f32[2048,128]{1,0:T(8,128)S(1)} %copy-done.14, ...), custom_call_target="tpu_custom_call" | custom-call | flops 32768 | bytes 98304 | tf_op jit(solution)/shard_map/choose_panel/pallas_call | solution.py:129
  105.9 1.5 exchange.11
  107.4 1.8 products.21
  109.7 3.6 %collective-permute-start.18 = (f32[128,1024]{1,0:T(8,128)S(1)}, f32[128,1024]{1,0:T(8,128)S(1)}, u32[]{:S(2)}, u32[]{:S(2)}) collective-permute-start(f32[128,1024]{1,0:T(8,128)S(1)} %get-tuple-element.105), channel_id=1, source_target_pairs={{0,8},{4,12},{8,0},{12,4},{16,24},{20,28},{24,16},{28,20},{1,9},{5... | collective-permute-start | bytes 1572872 | tf_op jit(solution)/shard_map/ppermute | solution.py:422
  114.0 1.8 products.20
  115.9 1.5 collective-permute-done.15.refs_1_
  117.4 8.1 %collective-permute-done.18.refs_6_ = f32[128,1024]{1,0:T(8,128)S(1)} collective-permute-done((f32[128,1024]{1,0:T(8,128)S(1)}, f32[128,1024]{1,0:T(8,128)S(1)}, u32[]{:S(2)}, u32[]{:S(2)}) %collective-permute-start.18) | collective-permute-done | bytes 524320 | tf_op jit(solution)/shard_map/ppermute | solution.py:422
  125.5 1.3 exchange.12
  128.4 3.7 %collective-permute-start.22 = (f32[128,1280]{1,0:T(8,128)}, f32[128,1280]{1,0:T(8,128)S(1)}, u32[]{:S(2)}, u32[]{:S(2)}) collective-permute-start(f32[128,1280]{1,0:T(8,128)} %get-tuple-element.114), channel_id=1, source_target_pairs={{0,8},{4,12},{8,0},{12,4},{16,24},{20,28},{24,16},{28,20},{1,9},{5... | collective-permute-start | bytes 1966088 | tf_op jit(solution)/shard_map/ppermute | solution.py:422
  132.1 1.5 collective-permute-start.23
  133.7 3.7 %choose_panel.9 = (bf16[2048,256]{1,0:T(8,128)(2,1)S(1)}, bf16[2048,256]{1,0:T(8,128)(2,1)S(1)}, bf16[512,2048]{1,0:T(8,128)(2,1)S(1)}) custom-call(s32[2]{0:T(128)S(1)} %broadcast_select_fusion.3.which_ref, f32[2048,128]{1,0:T(8,128)} %collective-permute-done.1.refs_0_, f32[2048,128]{1,0:T(8,128)} %collective-permute-done.3.refs_1_, ...), custom_call_target="tpu_custom_call" | custom-call | flops 32768 | bytes 98304 | tf_op jit(solution)/shard_map/choose_panel/pallas_call | solution.py:129
  137.4 3.4 %copy-done.4 = bf16[2048,2048]{1,0:T(8,128)(2,1)S(1)} copy-done((bf16[2048,2048]{1,0:T(8,128)(2,1)S(1)}, bf16[2048,2048]{1,0:T(8,128)(2,1)}, u32[]{:S(2)}) %copy-start.4) | copy-done | bytes 8388632
  140.8 3.4 %copy-done.9 = bf16[2048,2048]{1,0:T(8,128)(2,1)S(1)} copy-done((bf16[2048,2048]{1,0:T(8,128)(2,1)S(1)}, bf16[2048,2048]{1,0:T(8,128)(2,1)}, u32[]{:S(2)}) %copy-start.9) | copy-done | bytes 8388632
  144.2 1.8 products.23
  146.0 1.8 products.22
  148.4 1.2 collective-permute-done.20.refs_1_
  149.6 1.5 exchange.13
  152.6 3.7 %collective-permute-start.27 = (f32[128,1024]{1,0:T(8,128)S(1)}, f32[128,1024]{1,0:T(8,128)S(1)}, u32[]{:S(2)}, u32[]{:S(2)}) collective-permute-start(f32[128,1024]{1,0:T(8,128)S(1)} %get-tuple-element.123), channel_id=1, source_target_pairs={{0,8},{4,12},{8,0},{12,4},{16,24},{20,28},{24,16},{28,20},{1,9},{5... | collective-permute-start | bytes 1572872 | tf_op jit(solution)/shard_map/ppermute | solution.py:422
  156.3 1.8 products.25
  158.2 1.8 products.24
  160.5 1.2 collective-permute-done.25.refs_1_
  161.7 6.8 %collective-permute-done.27.refs_4_ = f32[128,1024]{1,0:T(8,128)S(1)} collective-permute-done((f32[128,1024]{1,0:T(8,128)S(1)}, f32[128,1024]{1,0:T(8,128)S(1)}, u32[]{:S(2)}, u32[]{:S(2)}) %collective-permute-start.27) | collective-permute-done | bytes 524320 | tf_op jit(solution)/shard_map/ppermute | solution.py:422
  168.8 3.6 %collective-permute-start.29 = (f32[128,1280]{1,0:T(8,128)S(1)}, f32[128,1280]{1,0:T(8,128)S(1)}, u32[]{:S(2)}, u32[]{:S(2)}) collective-permute-start(f32[128,1280]{1,0:T(8,128)S(1)} %get-tuple-element.126), channel_id=1, source_target_pairs={{0,8},{4,12},{8,0},{12,4},{16,24},{20,28},{24,16},{28,20},{1,9},{5... | collective-permute-start | bytes 1966088 | tf_op jit(solution)/shard_map/ppermute | solution.py:422
  173.1 13.8 %collective-permute-done.29.refs_0_ = f32[128,1280]{1,0:T(8,128)S(1)} collective-permute-done((f32[128,1280]{1,0:T(8,128)S(1)}, f32[128,1280]{1,0:T(8,128)S(1)}, u32[]{:S(2)}, u32[]{:S(2)}) %collective-permute-start.29) | collective-permute-done | bytes 655392 | tf_op jit(solution)/shard_map/ppermute | solution.py:422
  189.7 1.8 collective-permute-start.32
  191.5 1.5 collective-permute-start.33
  193.8 1.7 collective-permute-start.40
  195.7 1.3 collective-permute-start.39
  197.5 7.0 %collective-permute-done.32.refs_0_ = f32[128,1024]{1,0:T(8,128)} collective-permute-done((f32[128,1024]{1,0:T(8,128)}, f32[128,1024]{1,0:T(8,128)}, u32[]{:S(2)}, u32[]{:S(2)}) %collective-permute-start.32) | collective-permute-done | bytes 524320 | tf_op jit(solution)/shard_map/ppermute | solution.py:422
  207.1 1.5 exchange.16
  208.9 3.5 %collective-permute-start.34 = (f32[128,1024]{1,0:T(8,128)S(1)}, f32[128,1024]{1,0:T(8,128)S(1)}, u32[]{:S(2)}, u32[]{:S(2)}) collective-permute-start(f32[128,1024]{1,0:T(8,128)S(1)} %get-tuple-element.134), channel_id=1, source_target_pairs={{0,8},{4,12},{8,0},{12,4},{16,24},{20,28},{24,16},{28,20},{1,9},{5... | collective-permute-start | bytes 1572872 | tf_op jit(solution)/shard_map/ppermute | solution.py:422
  221.0 17.9 %update.2.refs_2_.refs_15_ = f32[2048,2048]{1,0:T(8,128)} custom-call(s32[6]{0:T(128)S(1)} %broadcast_select_fusion.4.place_ref, f32[128,1024]{1,0:T(8,128)S(1)} %copy-done.28, f32[128,1024]{1,0:T(8,128)S(1)} %collective-permute-done.35.refs_1_, f32[128,1024]{1,0:T(8,128)S(1)} %copy-done.32, f32[128,1024]{1,0:T(8,128)S(1)} %collective-permute-done.36.refs_3_, ...), custom_call_target="tpu_custom_call" | custom-call | flops 150994944 | bytes 360448 | tf_op jit(solution)/shard_map/update/pallas_call | solution.py:215
  238.9 5.8 %copy-done.11 = f32[2048,2048]{1,0:T(8,128)S(1)} copy-done((f32[2048,2048]{1,0:T(8,128)S(1)}, f32[2048,2048]{1,0:T(8,128)}, u32[]{:S(2)}) %copy-start.11) | copy-done | bytes 16777240
  245.3 1.5 collective-permute-done.41.refs_5_
  246.8 17.9 %update.3 = f32[2048,2048]{1,0:T(8,128)} custom-call(s32[6]{0:T(128)S(1)} %broadcast_select_fusion.4.place_ref, f32[128,1024]{1,0:T(8,128)S(1)} %copy-done.30, f32[128,1024]{1,0:T(8,128)S(1)} %collective-permute-done.24.refs_1_, f32[128,1280]{1,0:T(8,128)S(1)} %get-tuple-element.130.refs_2_, ...), custom_call_target="tpu_custom_call", output_to_operand_aliasing={{}: (16, {})} | custom-call | flops 150994944 | bytes 360448 | tf_op jit(solution)/shard_map/update/pallas_call | solution.py:215
  (194 shorter events, 34.0 us)
Async XLA Ops:
  0.0 7.8 %copy-start.46 = (s32[3]{0:T(128)S(1)}, s32[3]{0:T(128)}, u32[]{:S(2)}) copy-start(s32[3]{0:T(128)} %param.14) | copy-start | bytes 40
  0.0 7.8 %copy-start.54 = (s32[4,2]{1,0:T(4,128)S(1)}, s32[4,2]{1,0:T(4,128)}, u32[]{:S(2)}) copy-start(s32[4,2]{1,0:T(4,128)} %constant.99.clone) | copy-start | bytes 100
  2.7 13.5 %copy-start.15 = (f32[2048,128]{1,0:T(8,128)}, f32[2048,128]{1,0:T(8,128)S(1)}, u32[]{:S(2)}) copy-start(f32[2048,128]{1,0:T(8,128)S(1)} %get-tuple-element.146.refs_0_) | copy-start | bytes 3145732
  2.7 26.9 %collective-permute-start.5 = (f32[2048,128]{1,0:T(8,128)S(1)}, f32[2048,128]{1,0:T(8,128)S(1)}, u32[]{:S(2)}, u32[]{:S(2)}) collective-permute-start(f32[2048,128]{1,0:T(8,128)S(1)} %get-tuple-element.146.refs_0_), channel_id=1, source_target_pairs={{0,1},{1,0},{2,3},{3,2},{4,5},{5,4},{6,7},{7,6},{8,9},{9,8},{10,11... | collective-permute-start | bytes 3145736 | tf_op jit(solution)/shard_map/ppermute | solution.py:271
  5.7 26.2 %collective-permute-start = (f32[2048,128]{1,0:T(8,128)S(1)}, f32[2048,128]{1,0:T(8,128)}, u32[]{:S(2)}, u32[]{:S(2)}) collective-permute-start(f32[2048,128]{1,0:T(8,128)S(1)} %get-tuple-element.146.refs_0_), channel_id=1, source_target_pairs={{0,2},{1,3},{2,0},{3,1},{4,6},{5,7},{6,4},{7,5},{8,10},{9,11},{10,... | collective-permute-start | bytes 3145736 | tf_op jit(solution)/shard_map/ppermute | solution.py:271
  7.2 62.0 %collective-permute-start.4 = (f32[2048,128]{1,0:T(8,128)}, f32[2048,128]{1,0:T(8,128)}, u32[]{:S(2)}, u32[]{:S(2)}) collective-permute-start(f32[2048,128]{1,0:T(8,128)} %get-tuple-element.145.refs_1_), channel_id=1, source_target_pairs={{0,2},{1,3},{2,0},{3,1},{4,6},{5,7},{6,4},{7,5},{8,10},{9,11},{10,... | collective-permute-start | bytes 3145736 | tf_op jit(solution)/shard_map/ppermute | solution.py:271
  7.7 61.5 %collective-permute-start.2 = (f32[2048,128]{1,0:T(8,128)}, f32[2048,128]{1,0:T(8,128)}, u32[]{:S(2)}, u32[]{:S(2)}) collective-permute-start(f32[2048,128]{1,0:T(8,128)} %get-tuple-element.145.refs_1_), channel_id=1, source_target_pairs={{0,1},{1,0},{2,3},{3,2},{4,5},{5,4},{6,7},{7,6},{8,9},{9,8},{10,11... | collective-permute-start | bytes 3145736 | tf_op jit(solution)/shard_map/ppermute | solution.py:271
  8.0 5.8 %copy-start.10 = (f32[2048,2048]{1,0:T(8,128)S(1)}, f32[2048,2048]{1,0:T(8,128)}, u32[]{:S(2)}) copy-start(f32[2048,2048]{1,0:T(8,128)} %refs_14_.3) | copy-start | bytes 50331652
  16.2 23.3 %copy-start = (bf16[2048,2048]{1,0:T(8,128)(2,1)}, bf16[2048,2048]{1,0:T(8,128)(2,1)S(1)}, u32[]{:S(2)}) copy-start(bf16[2048,2048]{1,0:T(8,128)(2,1)S(1)} %get-tuple-element.76.high_ref) | copy-start | bytes 25165828
  16.2 23.3 %copy-start.5 = (bf16[2048,2048]{1,0:T(8,128)(2,1)}, bf16[2048,2048]{1,0:T(8,128)(2,1)S(1)}, u32[]{:S(2)}) copy-start(bf16[2048,2048]{1,0:T(8,128)(2,1)S(1)} %get-tuple-element.77.low_ref) | copy-start | bytes 25165828
  39.4 3.1 %collective-permute-start.7 = (f32[128,512]{1,0:T(8,128)S(1)}, f32[128,512]{1,0:T(8,128)S(1)}, u32[]{:S(2)}, u32[]{:S(2)}) collective-permute-start(f32[128,512]{1,0:T(8,128)S(1)} %get-tuple-element.81), channel_id=1, source_target_pairs={{0,4},{4,0},{8,12},{12,8},{16,20},{20,16},{24,28},{28,24},{1,5},{5... | collective-permute-start | bytes 786440 | tf_op jit(solution)/shard_map/ppermute | solution.py:241
  42.0 1.9 collective-permute-start.6
  46.5 15.9 %collective-permute-start.10 = (f32[128,1024]{1,0:T(8,128)}, f32[128,1024]{1,0:T(8,128)S(1)}, u32[]{:S(2)}, u32[]{:S(2)}) collective-permute-start(f32[128,1024]{1,0:T(8,128)} %get-tuple-element.87), channel_id=1, source_target_pairs={{0,8},{4,12},{8,0},{12,4},{16,24},{20,28},{24,16},{28,20},{1,9},{5... | collective-permute-start | bytes 1572872 | tf_op jit(solution)/shard_map/ppermute | solution.py:422
  57.3 3.7 %copy-start.47 = (s32[4,2]{1,0:T(4,128)S(1)}, s32[4,2]{1,0:T(4,128)}, u32[]{:S(2)}) copy-start(s32[4,2]{1,0:T(4,128)} %constant.101.clone) | copy-start | bytes 100
  57.3 3.7 %copy-start.48 = (s32[4,2]{1,0:T(4,128)S(1)}, s32[4,2]{1,0:T(4,128)}, u32[]{:S(2)}) copy-start(s32[4,2]{1,0:T(4,128)} %constant.100.clone) | copy-start | bytes 100
  57.3 3.8 %collective-permute-start.9 = (f32[128,512]{1,0:T(8,128)}, f32[128,512]{1,0:T(8,128)}, u32[]{:S(2)}, u32[]{:S(2)}) collective-permute-start(f32[128,512]{1,0:T(8,128)} %get-tuple-element.86), channel_id=1, source_target_pairs={{0,4},{4,0},{8,12},{12,8},{16,20},{20,16},{24,28},{28,24},{1,5},{5... | collective-permute-start | bytes 786440 | tf_op jit(solution)/shard_map/ppermute | solution.py:241
  60.6 1.8 collective-permute-start.8
  67.3 38.5 %collective-permute-start.13 = (f32[128,1024]{1,0:T(8,128)}, f32[128,1024]{1,0:T(8,128)S(1)}, u32[]{:S(2)}, u32[]{:S(2)}) collective-permute-start(f32[128,1024]{1,0:T(8,128)} %get-tuple-element.94), channel_id=1, source_target_pairs={{0,8},{4,12},{8,0},{12,4},{16,24},{20,28},{24,16},{28,20},{1,9},{5... | collective-permute-start | bytes 1572872 | tf_op jit(solution)/shard_map/ppermute | solution.py:422
  67.8 38.1 %collective-permute-start.14 = (f32[128,1024]{1,0:T(8,128)}, f32[128,1024]{1,0:T(8,128)}, u32[]{:S(2)}, u32[]{:S(2)}) collective-permute-start(f32[128,1024]{1,0:T(8,128)} %get-tuple-element.95.refs_6_), channel_id=1, source_target_pairs={{8,16},{12,20},{16,8},{20,12},{9,17},{13,21},{17,9},{21,13},{10,18... | collective-permute-start | bytes 1572872 | tf_op jit(solution)/shard_map/ppermute | solution.py:427
  85.5 12.1 %collective-permute-start.12 = (f32[128,512]{1,0:T(8,128)}, f32[128,512]{1,0:T(8,128)}, u32[]{:S(2)}, u32[]{:S(2)}) collective-permute-start(f32[128,512]{1,0:T(8,128)} %get-tuple-element.93), channel_id=1, source_target_pairs={{0,4},{4,0},{8,12},{12,8},{16,20},{20,16},{24,28},{28,24},{1,5},{5... | collective-permute-start | bytes 786440 | tf_op jit(solution)/shard_map/ppermute | solution.py:241
  96.7 9.0 %collective-permute-start.11 = (f32[128,512]{1,0:T(8,128)S(1)}, f32[128,512]{1,0:T(8,128)S(1)}, u32[]{:S(2)}, u32[]{:S(2)}) collective-permute-start(f32[128,512]{1,0:T(8,128)S(1)} %get-tuple-element.91), channel_id=1, source_target_pairs={{0,4},{4,0},{8,12},{12,8},{16,20},{20,16},{24,28},{28,24},{1,5},{5... | collective-permute-start | bytes 786440 | tf_op jit(solution)/shard_map/ppermute | solution.py:241
  97.2 36.4 %collective-permute-start.3 = (f32[2048,128]{1,0:T(8,128)}, f32[2048,128]{1,0:T(8,128)}, u32[]{:S(2)}, u32[]{:S(2)}) collective-permute-start(f32[2048,128]{1,0:T(8,128)} %collective-permute-done.2.refs_1_.refs_3_.refs_2_), channel_id=1, source_target_pairs={{0,2},{1,3},{2,0},{3,1},{4,6},{5,7},{6,4},{7,5},{8,10},{9,11},{10,... | collective-permute-start | bytes 3145736 | tf_op jit(solution)/shard_map/ppermute | solution.py:271
  97.6 36.0 %collective-permute-start.1 = (f32[2048,128]{1,0:T(8,128)}, f32[2048,128]{1,0:T(8,128)}, u32[]{:S(2)}, u32[]{:S(2)}) collective-permute-start(f32[2048,128]{1,0:T(8,128)} %collective-permute-done.refs_3_.refs_2_.refs_4_), channel_id=1, source_target_pairs={{0,1},{1,0},{2,3},{3,2},{4,5},{5,4},{6,7},{7,6},{8,9},{9,8},{10,11... | collective-permute-start | bytes 3145736 | tf_op jit(solution)/shard_map/ppermute | solution.py:271
  98.2 9.2 %slice-start = ((s8[8388608]{0:T(1024)(128)(4,1)}), s8[4194304]{0:T(1024)(128)(4,1)S(1)}, s32[]{:S(2)}) async-start(s8[8388608]{0:T(1024)(128)(4,1)} %bitcast.37), calls=%async_computation | async-start | bytes 8388608
  101.1 6.3 %slice-start.1 = ((s8[8388608]{0:T(1024)(128)(4,1)}), s8[4194304]{0:T(1024)(128)(4,1)S(1)}, s32[]{:S(2)}) async-start(s8[8388608]{0:T(1024)(128)(4,1)} %bitcast.37), calls=%async_computation.1 | async-start | bytes 8388608
  105.8 7.6 %collective-permute-start.17 = (f32[128,256]{1,0:T(8,128)S(1)}, f32[128,256]{1,0:T(8,128)S(1)}, u32[]{:S(2)}, u32[]{:S(2)}) collective-permute-start(f32[128,256]{1,0:T(8,128)S(1)} %get-tuple-element.104), channel_id=1, source_target_pairs={{0,4},{4,0},{8,12},{12,8},{16,20},{20,16},{24,28},{28,24},{1,5},{5... | collective-permute-start | bytes 393224 | tf_op jit(solution)/shard_map/ppermute | solution.py:241
  109.2 6.6 %collective-permute-start.16 = (f32[128,512]{1,0:T(8,128)S(1)}, f32[128,512]{1,0:T(8,128)S(1)}, u32[]{:S(2)}, u32[]{:S(2)}) collective-permute-start(f32[128,512]{1,0:T(8,128)S(1)} %get-tuple-element.103), channel_id=1, source_target_pairs={{0,4},{4,0},{8,12},{12,8},{16,20},{20,16},{24,28},{28,24},{1,5},{5... | collective-permute-start | bytes 786440 | tf_op jit(solution)/shard_map/ppermute | solution.py:241
  109.7 15.8 %collective-permute-start.18 = (f32[128,1024]{1,0:T(8,128)S(1)}, f32[128,1024]{1,0:T(8,128)S(1)}, u32[]{:S(2)}, u32[]{:S(2)}) collective-permute-start(f32[128,1024]{1,0:T(8,128)S(1)} %get-tuple-element.105), channel_id=1, source_target_pairs={{0,8},{4,12},{8,0},{12,4},{16,24},{20,28},{24,16},{28,20},{1,9},{5... | collective-permute-start | bytes 1572872 | tf_op jit(solution)/shard_map/ppermute | solution.py:422
  113.3 12.2 %collective-permute-start.19 = (f32[128,1024]{1,0:T(8,128)S(1)}, f32[128,1024]{1,0:T(8,128)S(1)}, u32[]{:S(2)}, u32[]{:S(2)}) collective-permute-start(f32[128,1024]{1,0:T(8,128)S(1)} %get-tuple-element.106.refs_8_), channel_id=1, source_target_pairs={{8,16},{12,20},{16,8},{20,12},{9,17},{13,21},{17,9},{21,13},{10,18... | collective-permute-start | bytes 1572872 | tf_op jit(solution)/shard_map/ppermute | solution.py:427
  115.8 1.6 collective-permute-start.15
  128.4 21.1 %collective-permute-start.22 = (f32[128,1280]{1,0:T(8,128)}, f32[128,1280]{1,0:T(8,128)S(1)}, u32[]{:S(2)}, u32[]{:S(2)}) collective-permute-start(f32[128,1280]{1,0:T(8,128)} %get-tuple-element.114), channel_id=1, source_target_pairs={{0,8},{4,12},{8,0},{12,4},{16,24},{20,28},{24,16},{28,20},{1,9},{5... | collective-permute-start | bytes 1966088 | tf_op jit(solution)/shard_map/ppermute | solution.py:422
  132.1 17.4 %collective-permute-start.23 = (f32[128,1024]{1,0:T(8,128)}, f32[128,1024]{1,0:T(8,128)}, u32[]{:S(2)}, u32[]{:S(2)}) collective-permute-start(f32[128,1024]{1,0:T(8,128)} %get-tuple-element.115.refs_6_), channel_id=1, source_target_pairs={{8,16},{12,20},{16,8},{20,12},{9,17},{13,21},{17,9},{21,13},{10,18... | collective-permute-start | bytes 1572872 | tf_op jit(solution)/shard_map/ppermute | solution.py:427
  145.9 3.6 %copy-start.34 = (f32[128,1024]{1,0:T(8,128)S(1)}, f32[128,1024]{1,0:T(8,128)}, u32[]{:S(2)}) copy-start(f32[128,1024]{1,0:T(8,128)} %copy-done.33) | copy-start | bytes 1572868
  146.0 2.4 collective-permute-start.21
  147.8 1.7 collective-permute-start.20
  151.9 16.6 %collective-permute-start.28 = (f32[128,1280]{1,0:T(8,128)S(1)}, f32[128,1280]{1,0:T(8,128)S(1)}, u32[]{:S(2)}, u32[]{:S(2)}) collective-permute-start(f32[128,1280]{1,0:T(8,128)S(1)} %get-tuple-element.124.refs_6_), channel_id=1, source_target_pairs={{8,16},{12,20},{16,8},{20,12},{9,17},{13,21},{17,9},{21,13},{10,18... | collective-permute-start | bytes 1966088 | tf_op jit(solution)/shard_map/ppermute | solution.py:427
  152.6 15.9 %collective-permute-start.27 = (f32[128,1024]{1,0:T(8,128)S(1)}, f32[128,1024]{1,0:T(8,128)S(1)}, u32[]{:S(2)}, u32[]{:S(2)}) collective-permute-start(f32[128,1024]{1,0:T(8,128)S(1)} %get-tuple-element.123), channel_id=1, source_target_pairs={{0,8},{4,12},{8,0},{12,4},{16,24},{20,28},{24,16},{28,20},{1,9},{5... | collective-permute-start | bytes 1572872 | tf_op jit(solution)/shard_map/ppermute | solution.py:422
  158.1 2.4 collective-permute-start.26
  160.0 1.7 collective-permute-start.25
  168.8 18.1 %copy-start.31 = (f32[128,1024]{1,0:T(8,128)}, f32[128,1024]{1,0:T(8,128)S(1)}, u32[]{:S(2)}) copy-start(f32[128,1024]{1,0:T(8,128)S(1)} %get-tuple-element.137.refs_2_) | copy-start | bytes 1572868
  168.8 20.7 %copy-start.49 = (s32[4,6]{1,0:T(4,128)S(1)}, s32[4,6]{1,0:T(4,128)}, u32[]{:S(2)}) copy-start(s32[4,6]{1,0:T(4,128)} %constant.103.clone) | copy-start | bytes 292
  168.8 20.7 %copy-start.50 = (s32[4,6]{1,0:T(4,128)S(1)}, s32[4,6]{1,0:T(4,128)}, u32[]{:S(2)}) copy-start(s32[4,6]{1,0:T(4,128)} %constant.102.clone) | copy-start | bytes 292
  168.8 18.0 %collective-permute-start.29 = (f32[128,1280]{1,0:T(8,128)S(1)}, f32[128,1280]{1,0:T(8,128)S(1)}, u32[]{:S(2)}, u32[]{:S(2)}) collective-permute-start(f32[128,1280]{1,0:T(8,128)S(1)} %get-tuple-element.126), channel_id=1, source_target_pairs={{0,8},{4,12},{8,0},{12,4},{16,24},{20,28},{24,16},{28,20},{1,9},{5... | collective-permute-start | bytes 1966088 | tf_op jit(solution)/shard_map/ppermute | solution.py:422
  172.4 0.7 collective-permute-start.30
  188.7 20.0 %copy-start.51 = (s32[2,3]{1,0:T(2,128)S(1)}, s32[2,3]{1,0:T(2,128)}, u32[]{:S(2)}) copy-start(s32[2,3]{1,0:T(2,128)} %constant.106.clone) | copy-start | bytes 76
  189.5 3.5 %collective-permute-start.31 = (f32[128,1280]{1,0:T(8,128)S(1)}, f32[128,1280]{1,0:T(8,128)S(1)}, u32[]{:S(2)}, u32[]{:S(2)}) collective-permute-start(f32[128,1280]{1,0:T(8,128)S(1)} %get-tuple-element.130.refs_2_), channel_id=1, source_target_pairs={{0,4},{4,0},{8,12},{12,8},{16,20},{20,16},{24,28},{28,24},{1,5},{5... | collective-permute-start | bytes 1966088 | tf_op jit(solution)/shard_map/ppermute | solution.py:241
  189.7 14.7 %collective-permute-start.32 = (f32[128,1024]{1,0:T(8,128)}, f32[128,1024]{1,0:T(8,128)}, u32[]{:S(2)}, u32[]{:S(2)}) collective-permute-start(f32[128,1024]{1,0:T(8,128)} %copy-done.45), channel_id=1, source_target_pairs={{0,8},{4,12},{8,0},{12,4},{16,24},{20,28},{24,16},{28,20},{1,9},{5... | collective-permute-start | bytes 1572872 | tf_op jit(solution)/shard_map/ppermute | solution.py:422
  191.5 12.9 %collective-permute-start.33 = (f32[128,1024]{1,0:T(8,128)}, f32[128,1024]{1,0:T(8,128)}, u32[]{:S(2)}, u32[]{:S(2)}) collective-permute-start(f32[128,1024]{1,0:T(8,128)} %copy-done.35), channel_id=1, source_target_pairs={{8,16},{12,20},{16,8},{20,12},{9,17},{13,21},{17,9},{21,13},{10,18... | collective-permute-start | bytes 1572872 | tf_op jit(solution)/shard_map/ppermute | solution.py:427
  193.8 14.8 %collective-permute-start.40 = (f32[256,256]{1,0:T(8,128)}, f32[256,256]{1,0:T(8,128)}, u32[]{:S(2)}, u32[]{:S(2)}) collective-permute-start(f32[256,256]{1,0:T(8,128)} %maximum_select_fusion), channel_id=1, source_target_pairs={{0,3},{1,2},{2,1},{3,0},{4,7},{5,6},{6,5},{7,4},{8,11},{9,10},{10,... | collective-permute-start | bytes 786440 | tf_op jit(solution)/shard_map/ppermute | solution.py:438
  195.7 13.2 %collective-permute-start.39 = (f32[256,256]{1,0:T(8,128)}, f32[256,256]{1,0:T(8,128)S(1)}, u32[]{:S(2)}, u32[]{:S(2)}) collective-permute-start(f32[256,256]{1,0:T(8,128)} %maximum_select_fusion), channel_id=1, source_target_pairs={{0,2},{1,3},{2,0},{3,1},{4,6},{5,7},{6,4},{7,5},{8,10},{9,11},{10,... | collective-permute-start | bytes 786440 | tf_op jit(solution)/shard_map/ppermute | solution.py:438
  196.9 21.6 %collective-permute-start.38 = (f32[256,256]{1,0:T(8,128)}, f32[256,256]{1,0:T(8,128)S(1)}, u32[]{:S(2)}, u32[]{:S(2)}) collective-permute-start(f32[256,256]{1,0:T(8,128)} %maximum_select_fusion), channel_id=1, source_target_pairs={{0,1},{1,0},{2,3},{3,2},{4,5},{5,4},{6,7},{7,6},{8,9},{9,8},{10,11... | collective-permute-start | bytes 786440 | tf_op jit(solution)/shard_map/ppermute | solution.py:438
  204.5 15.4 %collective-permute-start.35 = (f32[128,1024]{1,0:T(8,128)}, f32[128,1024]{1,0:T(8,128)S(1)}, u32[]{:S(2)}, u32[]{:S(2)}) collective-permute-start(f32[128,1024]{1,0:T(8,128)} %copy-done.27), channel_id=1, source_target_pairs={{0,4},{4,0},{8,12},{12,8},{16,20},{20,16},{24,28},{28,24},{1,5},{5... | collective-permute-start | bytes 1572872 | tf_op jit(solution)/shard_map/ppermute | solution.py:241
  204.5 15.4 %collective-permute-start.36 = (f32[128,1024]{1,0:T(8,128)}, f32[128,1024]{1,0:T(8,128)S(1)}, u32[]{:S(2)}, u32[]{:S(2)}) collective-permute-start(f32[128,1024]{1,0:T(8,128)} %copy-done.31), channel_id=1, source_target_pairs={{0,4},{4,0},{8,12},{12,8},{16,20},{20,16},{24,28},{28,24},{1,5},{5... | collective-permute-start | bytes 1572872 | tf_op jit(solution)/shard_map/ppermute | solution.py:241
  207.1 12.8 %copy-start.25 = (bf16[2048,256]{1,0:T(8,128)(2,1)S(1)}, bf16[2048,256]{1,0:T(8,128)(2,1)}, u32[]{:S(2)}) copy-start(bf16[2048,256]{1,0:T(8,128)(2,1)} %copy-done.24) | copy-start | bytes 3145732
  207.1 12.8 %copy-start.26 = (f32[3,256,256]{2,1,0:T(8,128)S(1)}, f32[3,256,256]{2,1,0:T(8,128)}, u32[]{:S(2)}) copy-start(f32[3,256,256]{2,1,0:T(8,128)} %refs_6_.3) | copy-start | bytes 2359300
  207.1 12.8 %copy-start.28 = (f32[128,1024]{1,0:T(8,128)S(1)}, f32[128,1024]{1,0:T(8,128)}, u32[]{:S(2)}) copy-start(f32[128,1024]{1,0:T(8,128)} %copy-done.27) | copy-start | bytes 1572868
  208.6 11.3 %copy-start.19 = (bf16[2048,256]{1,0:T(8,128)(2,1)S(1)}, bf16[2048,256]{1,0:T(8,128)(2,1)}, u32[]{:S(2)}) copy-start(bf16[2048,256]{1,0:T(8,128)(2,1)} %copy-done.18) | copy-start | bytes 3145732
  208.6 11.3 %copy-start.21 = (bf16[2048,256]{1,0:T(8,128)(2,1)S(1)}, bf16[2048,256]{1,0:T(8,128)(2,1)}, u32[]{:S(2)}) copy-start(bf16[2048,256]{1,0:T(8,128)(2,1)} %copy-done.20) | copy-start | bytes 3145732
  208.6 11.3 %copy-start.23 = (bf16[2048,256]{1,0:T(8,128)(2,1)S(1)}, bf16[2048,256]{1,0:T(8,128)(2,1)}, u32[]{:S(2)}) copy-start(bf16[2048,256]{1,0:T(8,128)(2,1)} %copy-done.22) | copy-start | bytes 3145732
  208.6 11.3 %collective-permute-start.37 = (f32[128,1024]{1,0:T(8,128)S(1)}, f32[128,1024]{1,0:T(8,128)S(1)}, u32[]{:S(2)}, u32[]{:S(2)}) collective-permute-start(f32[128,1024]{1,0:T(8,128)S(1)} %get-tuple-element.138.refs_4_), channel_id=1, source_target_pairs={{0,4},{4,0},{8,12},{12,8},{16,20},{20,16},{24,28},{28,24},{1,5},{5... | collective-permute-start | bytes 1572872 | tf_op jit(solution)/shard_map/ppermute | solution.py:241
  208.9 29.9 %collective-permute-start.34 = (f32[128,1024]{1,0:T(8,128)S(1)}, f32[128,1024]{1,0:T(8,128)S(1)}, u32[]{:S(2)}, u32[]{:S(2)}) collective-permute-start(f32[128,1024]{1,0:T(8,128)S(1)} %get-tuple-element.134), channel_id=1, source_target_pairs={{0,8},{4,12},{8,0},{12,4},{16,24},{20,28},{24,16},{28,20},{1,9},{5... | collective-permute-start | bytes 1572872 | tf_op jit(solution)/shard_map/ppermute | solution.py:422
  218.5 26.7 %collective-permute-start.24 = (f32[128,1024]{1,0:T(8,128)}, f32[128,1024]{1,0:T(8,128)S(1)}, u32[]{:S(2)}, u32[]{:S(2)}) collective-permute-start(f32[128,1024]{1,0:T(8,128)} %copy-done.29), channel_id=1, source_target_pairs={{0,4},{4,0},{8,12},{12,8},{16,20},{20,16},{24,28},{28,24},{1,5},{5... | collective-permute-start | bytes 1572872 | tf_op jit(solution)/shard_map/ppermute | solution.py:241
  238.9 5.8 %copy-start.11 = (f32[2048,2048]{1,0:T(8,128)S(1)}, f32[2048,2048]{1,0:T(8,128)}, u32[]{:S(2)}) copy-start(f32[2048,2048]{1,0:T(8,128)} %update.2.refs_2_.refs_15_) | copy-start | bytes 50331652
  244.7 2.1 collective-permute-start.41
  (35 other events, 63.0 us)
